TPU v7x, 32 devices: a whole 2x2x4 slice. The times are simulated.
32 devices in a mesh: member: 4 (over z), row: 4 (over y, core), col: 2 (over x).
Axes of the slice: x: 2, y: 2, z: 4, core: 2. Of those that a mesh axis runs over, the one named last changes fastest.
Arguments:
- pert: bfloat16 [4, 3, 2, 64, 1024], P('member', None, None, 'row', 'col'), may hold values from -6 to 6
- probes: bfloat16 [4, 3, 2, 64, 1024], P('member', None, None, 'row', 'col'), may hold values from -6 to 6
- diff_class: int32 [64, 1024], P('row', 'col'), may hold values from 0 to 7
- class_rate: float32 [8], replicated, may hold values from 0.03 to 0.24
Outputs:
- cov_probe: float32 [4, 3, 2, 64, 1024], P('member', None, None, 'row', 'col')
All inputs are finite; a program needn't handle non-finite values.
Results may differ from a plain program's by a relative error of at most 0.0018.
Values may be sent and summed in bfloat16 or wider, within the bound.
A program may use at most 128 MiB of HBM per device.

v0:
```python
import jax
import jax.numpy as jnp
from jax import lax
from jax.sharding import PartitionSpec as P

SWEEPS = 4


def extended(cells, sides, width):
    for axis, dim in sides:
        count = lax.axis_size(axis)
        ends = count - 1
        head = lax.slice_in_dim(cells, 0, width, axis=dim)
        tail = lax.slice_in_dim(cells, cells.shape[dim] - width, cells.shape[dim], axis=dim)
        cells = jnp.concatenate(
            [
                lax.ppermute(tail, axis, [(i, (i + 1) % count) for i in range(ends)]),
                cells,
                lax.ppermute(head, axis, [((i + 1) % count, i) for i in range(ends)]),
            ],
            axis=dim,
        )
    return cells


def class_rates(diff_class, class_rate):
    levels = jnp.arange(class_rate.shape[0], dtype=jnp.int32)
    picked = (diff_class[..., None] == levels).astype(jnp.float32)
    return jnp.sum(picked * class_rate, axis=-1)


def inside_mask(tile_rows, tile_cols, width):
    row_pos = lax.axis_index("row") * tile_rows + jnp.arange(
        -width, tile_rows + width, dtype=jnp.int32
    )
    col_pos = lax.axis_index("col") * tile_cols + jnp.arange(
        -width, tile_cols + width, dtype=jnp.int32
    )
    row_ok = (row_pos >= 0) & (row_pos < tile_rows * lax.axis_size("row"))
    col_ok = (col_pos >= 0) & (col_pos < tile_cols * lax.axis_size("col"))
    return (row_ok[:, None] & col_ok[None, :]).astype(jnp.float32)


def deep_diffuse(field_now, rate_wide, inside, width):
    for sweep_index in range(1, width + 1):
        center = field_now[..., 1:-1, 1:-1]
        beside_all = (
            field_now[..., 2:, 1:-1]
            + field_now[..., :-2, 1:-1]
            + field_now[..., 1:-1, 2:]
            + field_now[..., 1:-1, :-2]
        )
        row_stop = rate_wide.shape[0] - sweep_index
        col_stop = rate_wide.shape[1] - sweep_index
        local_rate = rate_wide[sweep_index:row_stop, sweep_index:col_stop]
        local_mask = inside[sweep_index:row_stop, sweep_index:col_stop]
        field_now = local_mask * (center + local_rate * (beside_all - 4.0 * center))
    return field_now


def body(pert, probes, diff_class, class_rate):
    cell_rate = class_rates(diff_class, class_rate)
    mem_local = pert.shape[0]
    tile_rows = pert.shape[3]
    tile_cols = pert.shape[4]
    total_members = mem_local * lax.axis_size("member")
    rate_wide = extended(cell_rate, (("row", 0), ("col", 1)), SWEEPS)
    stacked = jnp.concatenate([pert, probes], axis=0)
    wide_inputs = extended(stacked, (("row", 3), ("col", 4)), SWEEPS)
    pert_wide = wide_inputs[:mem_local]
    probe_wide = wide_inputs[mem_local:].astype(jnp.float32)
    inside = inside_mask(tile_rows, tile_cols, SWEEPS)
    member_piece = lax.all_gather(pert_wide, "member", axis=0, tiled=True)
    center_part = member_piece[:, :, :, SWEEPS : SWEEPS + tile_rows, SWEEPS : SWEEPS + tile_cols]
    field_now = member_piece[:, None].astype(jnp.float32) * probe_wide[None]
    field_now = deep_diffuse(field_now, rate_wide, inside, SWEEPS)
    summed = jnp.sum(center_part[:, None].astype(jnp.float32) * field_now, axis=0)
    return summed / (total_members - 1)


def solution(mesh):
    placed = (
        P("member", None, None, "row", "col"),
        P("member", None, None, "row", "col"),
        P("row", "col"),
        P(),
    )
    return jax.shard_map(
        body,
        mesh=mesh,
        in_specs=placed,
        out_specs=P("member", None, None, "row", "col"),
        check_vma=False,
    )
```

profile of v0, /device:TPU:0, one launch (start us, length us, event | category | flops | bytes accessed | tf_op | source)
XLA Modules:
  0.0 58.3 jit_solution(11158925013104716495)
XLA Ops:
  0.0 0.9 %constant_dynamic-update-slice_fusion.1 = bf16[2,3,2,16,512]{4,3,2,1,0:T(8,128)(2,1)S(1)} fusion(bf16[1,3,2,16,512]{4,3,2,1,0:T(8,128)(2,1)} %param.4), kind=kLoop, calls=%fused_computation.47 | loop fusion | bytes 196608
  0.9 0.9 %constant_dynamic-update-slice_fusion = bf16[2,3,2,16,512]{4,3,2,1,0:T(8,128)(2,1)S(1)} fusion(bf16[2,3,2,16,512]{4,3,2,1,0:T(8,128)(2,1)S(1)} %constant_dynamic-update-slice_fusion.1, bf16[1,3,2,16,512]{4,3,2,1,0:T(8,128)(2,1)} %param.5), kind=kLoop, calls=%fused_computation.46 | loop fusion | bytes 196608 | tf_op jit(solution)/shard_map/concatenate | solution.py:68
  1.8 2.4 %collective-permute-start = (bf16[2,3,2,4,512]{4,3,2,1,0:T(4,128)(2,1)S(1)}, bf16[2,3,2,4,512]{4,3,2,1,0:T(4,128)(2,1)S(1)}, u32[]{:S(2)}, u32[]{:S(2)}) collective-permute-start(bf16[2,3,2,4,512]{4,3,2,1,0:T(4,128)(2,1)S(1)} %get-tuple-element.9), channel_id=1, source_target_pairs={{0,2},{2,4},{4,6},{1,3},{3,5},{5,7},{8,10},{10,12},{12,14},{9,11},... | collective-permute-start | bytes 147464 | tf_op jit(solution)/shard_map/ppermute | solution.py:17
  4.2 1.3 %collective-permute-start.1 = (bf16[2,3,2,4,512]{4,3,2,1,0:T(4,128)(2,1)S(1)}, bf16[2,3,2,4,512]{4,3,2,1,0:T(4,128)(2,1)S(1)}, u32[]{:S(2)}, u32[]{:S(2)}) collective-permute-start(bf16[2,3,2,4,512]{4,3,2,1,0:T(4,128)(2,1)S(1)} %get-tuple-element.10), channel_id=1, source_target_pairs={{2,0},{4,2},{6,4},{3,1},{5,3},{7,5},{10,8},{12,10},{14,12},{11,9},... | collective-permute-start | bytes 147464 | tf_op jit(solution)/shard_map/ppermute | solution.py:19
  5.5 0.9 %select_reduce_fusion = f32[16,512]{1,0:T(8,128)S(1)} fusion(f32[8]{0:T(128)} %param.7, s32[16,512]{1,0:T(8,128)} %param.6), kind=kLoop, calls=%fused_computation.33 | loop fusion | flops 188416 | bytes 65568 | tf_op jit(solution)/shard_map/reduce_sum | solution.py:29
  6.5 5.2 %collective-permute-start.4 = (f32[4,512]{1,0:T(4,128)S(1)}, f32[4,512]{1,0:T(4,128)S(1)}, u32[]{:S(2)}, u32[]{:S(2)}) collective-permute-start(f32[4,512]{1,0:T(4,128)S(1)} %get-tuple-element.13), channel_id=1, source_target_pairs={{0,2},{2,4},{4,6},{1,3},{3,5},{5,7},{8,10},{10,12},{12,14},{9,11},... | collective-permute-start | bytes 24584 | tf_op jit(solution)/shard_map/ppermute | solution.py:17
  11.6 1.3 %collective-permute-start.5 = (f32[4,512]{1,0:T(4,128)S(1)}, f32[4,512]{1,0:T(4,128)S(1)}, u32[]{:S(2)}, u32[]{:S(2)}) collective-permute-start(f32[4,512]{1,0:T(4,128)S(1)} %get-tuple-element.14), channel_id=1, source_target_pairs={{2,0},{4,2},{6,4},{3,1},{5,3},{7,5},{10,8},{12,10},{14,12},{11,9},... | collective-permute-start | bytes 24584 | tf_op jit(solution)/shard_map/ppermute | solution.py:19
  13.0 0.1 and_convert_fusion
  13.0 0.1 slice.159
  13.1 0.1 slice.158
  13.2 0.1 slice.157
  13.3 0.1 slice.156
  13.4 2.6 %collective-permute-done.5 = f32[4,512]{1,0:T(4,128)S(1)} collective-permute-done((f32[4,512]{1,0:T(4,128)S(1)}, f32[4,512]{1,0:T(4,128)S(1)}, u32[]{:S(2)}, u32[]{:S(2)}) %collective-permute-start.5) | collective-permute-done | bytes 8224 | tf_op jit(solution)/shard_map/ppermute | solution.py:19
  16.0 3.4 %collective-permute-start.6 = (f32[24,4]{1,0:T(8,128)S(1)}, f32[24,4]{1,0:T(8,128)S(1)}, u32[]{:S(2)}, u32[]{:S(2)}) collective-permute-start(f32[24,4]{1,0:T(8,128)S(1)} %get-tuple-element.11), channel_id=1, source_target_pairs={{0,1},{2,3},{4,5},{6,7},{8,9},{10,11},{12,13},{14,15},{16,17},{18,... | collective-permute-start | bytes 1160 | tf_op jit(solution)/shard_map/ppermute | solution.py:17
  19.4 1.3 %collective-permute-start.7 = (f32[24,4]{1,0:T(8,128)S(1)}, f32[24,4]{1,0:T(8,128)S(1)}, u32[]{:S(2)}, u32[]{:S(2)}) collective-permute-start(f32[24,4]{1,0:T(8,128)S(1)} %get-tuple-element.12), channel_id=1, source_target_pairs={{1,0},{3,2},{5,4},{7,6},{9,8},{11,10},{13,12},{15,14},{17,16},{19,... | collective-permute-start | bytes 1160 | tf_op jit(solution)/shard_map/ppermute | solution.py:19
  20.7 0.1 pad_maximum_fusion.3
  20.8 4.5 %collective-permute-start.2 = (bf16[2,3,2,24,4]{4,3,2,1,0:T(8,128)(2,1)S(1)}, bf16[2,3,2,24,4]{4,3,2,1,0:T(8,128)(2,1)S(1)}, u32[]{:S(2)}, u32[]{:S(2)}) collective-permute-start(bf16[2,3,2,24,4]{4,3,2,1,0:T(8,128)(2,1)S(1)} %get-tuple-element.7), channel_id=1, source_target_pairs={{0,1},{2,3},{4,5},{6,7},{8,9},{10,11},{12,13},{14,15},{16,17},{18,... | collective-permute-start | bytes 6920 | tf_op jit(solution)/shard_map/ppermute | solution.py:17
  25.4 1.3 %collective-permute-start.3 = (bf16[2,3,2,24,4]{4,3,2,1,0:T(8,128)(2,1)S(1)}, bf16[2,3,2,24,4]{4,3,2,1,0:T(8,128)(2,1)S(1)}, u32[]{:S(2)}, u32[]{:S(2)}) collective-permute-start(bf16[2,3,2,24,4]{4,3,2,1,0:T(8,128)(2,1)S(1)} %get-tuple-element.8), channel_id=1, source_target_pairs={{1,0},{3,2},{5,4},{7,6},{9,8},{11,10},{13,12},{15,14},{17,16},{19,... | collective-permute-start | bytes 6920 | tf_op jit(solution)/shard_map/ppermute | solution.py:19
  26.7 0.1 pad_maximum_fusion.4
  26.8 0.1 slice.164
  26.9 0.1 slice.170
  27.0 0.1 slice.176
  27.1 0.3 collective-permute-done.2
  27.4 4.5 %collective-permute-done.3 = bf16[2,3,2,24,4]{4,3,2,1,0:T(8,128)(2,1)S(1)} collective-permute-done((bf16[2,3,2,24,4]{4,3,2,1,0:T(8,128)(2,1)S(1)}, bf16[2,3,2,24,4]{4,3,2,1,0:T(8,128)(2,1)S(1)}, u32[]{:S(2)}, u32[]{:S(2)}) %collective-permute-start.3) | collective-permute-done | bytes 2336 | tf_op jit(solution)/shard_map/ppermute | solution.py:19
  31.9 0.4 pad_maximum_fusion
  32.4 19.2 %all_gather.3 = bf16[4,3,2,24,520]{4,3,2,1,0:T(8,128)(2,1)S(1)} all-gather(bf16[1,3,2,24,520]{4,3,2,1,0:T(8,128)(2,1)S(1)} %get-tuple-element.6), channel_id=1, replica_groups=mesh['member'=4,'row'=4,'col'=2] {'member'}, dimensions={0}, use_global_device_ids=true | all-gather | bytes 748800 | tf_op jit(solution)/shard_map/all_gather | solution.py:73
  51.6 0.1 multiply_bitcast_fusion
  51.7 1.6 %fusion.11 = f32[4,1,3,2,22,518]{5,4,3,2,0,1:T(8,128)S(1)} fusion(f32[4,1,3,2,24,520]{5,4,3,2,0,1:T(8,128)S(1)} %multiply_bitcast_fusion, f32[22,518]{1,0:T(8,128)S(1)} %slice.164, f32[22,518]{1,0:T(8,128)S(1)} %slice.159), kind=kLoop, calls=%fused_computation.18 | loop fusion | flops 2188032 | bytes 6655264 | tf_op jit(solution)/shard_map/mul | solution.py:57
  53.3 1.6 %fusion.7 = f32[4,1,3,2,20,516]{5,4,3,2,0,1:T(8,128)S(1)} fusion(f32[4,1,3,2,22,518]{5,4,3,2,0,1:T(8,128)S(1)} %fusion.11, f32[20,516]{1,0:T(8,128)S(1)} %slice.170, f32[20,516]{1,0:T(8,128)S(1)} %slice.158), kind=kLoop, calls=%fused_computation.11 | loop fusion | flops 1981440 | bytes 6026880 | tf_op jit(solution)/shard_map/mul | solution.py:57
  54.9 1.6 %fusion.3 = f32[4,1,3,2,18,514]{5,4,3,2,0,1:T(8,128)S(1)} fusion(f32[4,1,3,2,20,516]{5,4,3,2,0,1:T(8,128)S(1)} %fusion.7, f32[18,514]{1,0:T(8,128)S(1)} %slice.176, f32[18,514]{1,0:T(8,128)S(1)} %slice.157), kind=kLoop, calls=%fused_computation.4 | loop fusion | flops 1776384 | bytes 5403168 | tf_op jit(solution)/shard_map/mul | solution.py:57
  56.5 1.0 %fusion.17 = f32[3,2,16,512]{3,2,1,0:T(8,128)S(1)} fusion(f32[4,1,3,2,18,514]{5,4,3,2,0,1:T(8,128)S(1)} %fusion.3, bf16[4,3,2,24,520]{4,3,2,1,0:T(8,128)(2,1)S(1)} %all_gather.3, f32[16,512]{1,0:T(8,128)S(1)} %select_reduce_fusion, f32[16,512]{1,0:T(8,128)S(1)} %slice.156), kind=kLoop, calls=%fused_computation.28 | loop fusion | flops 2113536 | bytes 4587520 | tf_op jit(solution)/shard_map/reduce_sum | solution.py:77
  57.6 0.7 %multiply_bitcast_fusion.1 = f32[1,3,2,16,512]{4,3,2,1,0:T(8,128)} fusion(f32[3,2,16,512]{3,2,1,0:T(8,128)S(1)} %fusion.17), kind=kLoop, calls=%fused_computation.35 | loop fusion | flops 49152 | bytes 393216 | tf_op jit(solution)/shard_map/div | solution.py:78
  (11 shorter events, 0.2 us)
Async XLA Ops:
  1.8 18.9 %collective-permute-start = (bf16[2,3,2,4,512]{4,3,2,1,0:T(4,128)(2,1)S(1)}, bf16[2,3,2,4,512]{4,3,2,1,0:T(4,128)(2,1)S(1)}, u32[]{:S(2)}, u32[]{:S(2)}) collective-permute-start(bf16[2,3,2,4,512]{4,3,2,1,0:T(4,128)(2,1)S(1)} %get-tuple-element.9), channel_id=1, source_target_pairs={{0,2},{2,4},{4,6},{1,3},{3,5},{5,7},{8,10},{10,12},{12,14},{9,11},... | collective-permute-start | bytes 147464 | tf_op jit(solution)/shard_map/ppermute | solution.py:17
  4.2 16.5 %collective-permute-start.1 = (bf16[2,3,2,4,512]{4,3,2,1,0:T(4,128)(2,1)S(1)}, bf16[2,3,2,4,512]{4,3,2,1,0:T(4,128)(2,1)S(1)}, u32[]{:S(2)}, u32[]{:S(2)}) collective-permute-start(bf16[2,3,2,4,512]{4,3,2,1,0:T(4,128)(2,1)S(1)} %get-tuple-element.10), channel_id=1, source_target_pairs={{2,0},{4,2},{6,4},{3,1},{5,3},{7,5},{10,8},{12,10},{14,12},{11,9},... | collective-permute-start | bytes 147464 | tf_op jit(solution)/shard_map/ppermute | solution.py:19
  6.5 6.9 %collective-permute-start.4 = (f32[4,512]{1,0:T(4,128)S(1)}, f32[4,512]{1,0:T(4,128)S(1)}, u32[]{:S(2)}, u32[]{:S(2)}) collective-permute-start(f32[4,512]{1,0:T(4,128)S(1)} %get-tuple-element.13), channel_id=1, source_target_pairs={{0,2},{2,4},{4,6},{1,3},{3,5},{5,7},{8,10},{10,12},{12,14},{9,11},... | collective-permute-start | bytes 24584 | tf_op jit(solution)/shard_map/ppermute | solution.py:17
  11.6 4.3 %collective-permute-start.5 = (f32[4,512]{1,0:T(4,128)S(1)}, f32[4,512]{1,0:T(4,128)S(1)}, u32[]{:S(2)}, u32[]{:S(2)}) collective-permute-start(f32[4,512]{1,0:T(4,128)S(1)} %get-tuple-element.14), channel_id=1, source_target_pairs={{2,0},{4,2},{6,4},{3,1},{5,3},{7,5},{10,8},{12,10},{14,12},{11,9},... | collective-permute-start | bytes 24584 | tf_op jit(solution)/shard_map/ppermute | solution.py:19
  16.0 10.7 %collective-permute-start.6 = (f32[24,4]{1,0:T(8,128)S(1)}, f32[24,4]{1,0:T(8,128)S(1)}, u32[]{:S(2)}, u32[]{:S(2)}) collective-permute-start(f32[24,4]{1,0:T(8,128)S(1)} %get-tuple-element.11), channel_id=1, source_target_pairs={{0,1},{2,3},{4,5},{6,7},{8,9},{10,11},{12,13},{14,15},{16,17},{18,... | collective-permute-start | bytes 1160 | tf_op jit(solution)/shard_map/ppermute | solution.py:17
  19.4 7.3 %collective-permute-start.7 = (f32[24,4]{1,0:T(8,128)S(1)}, f32[24,4]{1,0:T(8,128)S(1)}, u32[]{:S(2)}, u32[]{:S(2)}) collective-permute-start(f32[24,4]{1,0:T(8,128)S(1)} %get-tuple-element.12), channel_id=1, source_target_pairs={{1,0},{3,2},{5,4},{7,6},{9,8},{11,10},{13,12},{15,14},{17,16},{19,... | collective-permute-start | bytes 1160 | tf_op jit(solution)/shard_map/ppermute | solution.py:19
  20.8 6.5 %collective-permute-start.2 = (bf16[2,3,2,24,4]{4,3,2,1,0:T(8,128)(2,1)S(1)}, bf16[2,3,2,24,4]{4,3,2,1,0:T(8,128)(2,1)S(1)}, u32[]{:S(2)}, u32[]{:S(2)}) collective-permute-start(bf16[2,3,2,24,4]{4,3,2,1,0:T(8,128)(2,1)S(1)} %get-tuple-element.7), channel_id=1, source_target_pairs={{0,1},{2,3},{4,5},{6,7},{8,9},{10,11},{12,13},{14,15},{16,17},{18,... | collective-permute-start | bytes 6920 | tf_op jit(solution)/shard_map/ppermute | solution.py:17
  25.4 6.5 %collective-permute-start.3 = (bf16[2,3,2,24,4]{4,3,2,1,0:T(8,128)(2,1)S(1)}, bf16[2,3,2,24,4]{4,3,2,1,0:T(8,128)(2,1)S(1)}, u32[]{:S(2)}, u32[]{:S(2)}) collective-permute-start(bf16[2,3,2,24,4]{4,3,2,1,0:T(8,128)(2,1)S(1)} %get-tuple-element.8), channel_id=1, source_target_pairs={{1,0},{3,2},{5,4},{7,6},{9,8},{11,10},{13,12},{15,14},{17,16},{19,... | collective-permute-start | bytes 6920 | tf_op jit(solution)/shard_map/ppermute | solution.py:19
where the time goes:
time: 58.6 us; the launch traced here: 58.3 us
  starting transfers between devices  20.6 us (35%)
  blocking collectives  19.2 us (33%)
  other arithmetic  8.38 us (14%)
  waiting for transfers between devices  7.39 us (13%)
  local copies, waits for them, and re-layouts  2.43 us (4%)
    all_gather x1, blocking collectives, body(): member_piece = lax.all_gather(pert_wide, 'member', axis=0, tiled=True)  19.2 us
    ppermute x4, starting transfers between devices, extended(): lax.ppermute(tail, axis, [(i, (i + 1) % count) for i in range(ends)])  15.5 us
    ppermute x4, waiting for transfers between devices, extended(): lax.ppermute(head, axis, [((i + 1) % count, i) for i in range(ends)])  7.1 us
    ppermute x4, starting transfers between devices, extended(): lax.ppermute(head, axis, [((i + 1) % count, i) for i in range(ends)])  5.17 us
    mul x3, other arithmetic, deep_diffuse(): field_now = local_mask * (center + local_rate * (beside_all - 4.0 * center))  4.78 us
  transfers between devices with their start and end apart: 8, of which 3 were waited for; matrix products, arithmetic and copies ran while one was open for 3% of the time, Pallas kernels for 0%

commit v1 on v0

v1 whole, which is shorter than its diff:
```python
import functools

import jax
import jax.numpy as jnp
from jax import lax
from jax.experimental import pallas as pl
from jax.experimental.pallas import tpu as pltpu
from jax.sharding import PartitionSpec as P

SWEEPS = 4
MESH = pl.DeviceIdType.MESH
F32 = jnp.float32


def kernel(
    n, rows, cols,
    pert, probes, classes, rates, out,
    core, above, below, side, side_above, side_below,
    side_out, side_in, cls, cls_in, cls_above, cls_below,
    probe_field, keep, rate,
    z_send, z_recv, zs_send, zs_recv, y_send, y_recv, ys_send, ys_recv,
    x_send, x_recv, cx_send, cx_recv, cy_send, cy_recv,
):
    slabs, tile_rows, tile_cols = pert.shape
    pairs = slabs // 2
    half = tile_rows // 2
    wide = tile_cols + 128
    tall = tile_rows + half
    me = lax.axis_index("member")
    row = lax.axis_index("row")
    col = lax.axis_index("col")
    upper = (2 * me) // n

    def peer(step):
        mine = upper * (n - 1) + (1 - 2 * upper) * me
        other = step + (step + n - mine) // n
        return upper * (n - 1) + (1 - 2 * upper) * other

    has_up = (row + rows - 1) // rows
    has_down = 1 - (row + 1) // rows
    has_left = (col + cols - 1) // cols
    has_right = 1 - (col + 1) // cols
    sides = (
        (has_up, {"row": row - 1}),
        (has_down, {"row": row + 1}),
        (has_left, {"col": col - 1}),
        (has_right, {"col": col + 1}),
    )

    barrier = pltpu.get_barrier_semaphore()

    @pl.loop(0, n - 1)
    def _(step):
        pl.semaphore_signal(barrier, inc=1, device_id={"member": peer(step)}, device_id_type=MESH)

    for has, where in sides:
        @pl.when(has == 1)
        def _(where=where):
            pl.semaphore_signal(barrier, inc=1, device_id=where, device_id_type=MESH)

    def remote(src, dst, send, recv, where):
        return pltpu.make_async_remote_copy(
            src_ref=src, dst_ref=dst, send_sem=send, recv_sem=recv,
            device_id=where, device_id_type=MESH,
        )

    for which, slot in ((pert, me), (probes, n)):
        for pair in range(pairs):
            first = which[2 * pair].astype(F32)
            second = which[2 * pair + 1].astype(F32)
            for part in range(2):
                cut = slice(part * half, (part + 1) * half)
                core[slot, pair, part] = jnp.concatenate([first[cut], second[cut]], 0).astype(jnp.bfloat16)
    lane = lax.broadcasted_iota(jnp.int32, (tile_rows, 128), 1)
    for at, which in enumerate((pert, probes)):
        to_left = jnp.zeros((tile_rows, 128), F32)
        to_right = jnp.zeros((tile_rows, 128), F32)
        for slab in range(slabs):
            low = SWEEPS * slab
            head = which[slab, :, 0:128].astype(F32)
            tail = which[slab, :, tile_cols - 128 : tile_cols].astype(F32)
            if slab:
                head = pltpu.roll(head, low, 1)
                tail = pltpu.roll(tail, 128 - low, 1)
            to_left = jnp.where((lane >= low) & (lane < low + SWEEPS), head, to_left)
            to_right = jnp.where((lane >= 128 - SWEEPS - low) & (lane < 128 - low), tail, to_right)
        side_out[0, at] = to_left.astype(jnp.bfloat16)
        side_out[1, at] = to_right.astype(jnp.bfloat16)
    cls[:, 0:tile_cols] = classes[...]

    @pl.when(has_up == 0)
    def _():
        above[...] = jnp.zeros_like(above)
        side_above[...] = jnp.zeros_like(side_above)
        cls_above[...] = jnp.full_like(cls_above, -1)

    @pl.when(has_down == 0)
    def _():
        below[...] = jnp.zeros_like(below)
        side_below[...] = jnp.zeros_like(side_below)
        cls_below[...] = jnp.full_like(cls_below, -1)

    @pl.when(has_right == 0)
    def _():
        side_in[0] = jnp.zeros_like(side_in[0])
        cls_in[0] = jnp.full_like(cls_in[0], -1)

    @pl.when(has_left == 0)
    def _():
        side_in[1] = jnp.zeros_like(side_in[1])
        cls_in[1] = jnp.full_like(cls_in[1], -1)

    pl.semaphore_wait(barrier, n - 1 + has_up + has_down + has_left + has_right)

    def x_copies(at):
        where = sides[2 + at][1]
        block = (0, tile_cols - 128)[at]
        return (
            remote(side_out.at[at], side_in.at[at], x_send.at[at], x_recv.at[at], where),
            remote(classes.at[:, block : block + 128], cls_in.at[at], cx_send.at[at], cx_recv.at[at], where),
        )

    def z_copy(step):
        return remote(core.at[me], core.at[me], z_send.at[step], z_recv.at[me], {"member": peer(step)})

    def z_arrival(other):
        return remote(core.at[other], core.at[other], z_send.at[0], z_recv.at[other], {"member": other})

    def zs_copy(step):
        return remote(side.at[me], side.at[me], zs_send.at[step], zs_recv.at[me], {"member": peer(step)})

    def zs_arrival(other):
        return remote(side.at[other], side.at[other], zs_send.at[0], zs_recv.at[other], {"member": other})

    def y_copy(slot, at):
        return remote(
            core.at[slot, :, at], (below, above)[at].at[slot],
            y_send.at[slot, at], y_recv.at[slot, at], sides[at][1],
        )

    def ys_copy(slot, at):
        return remote(
            side.at[slot], (side_below, side_above)[at].at[slot],
            ys_send.at[slot, at], ys_recv.at[slot, at], sides[at][1],
        )

    def cy_copy(at):
        return remote(
            cls.at[at * half : (at + 1) * half], (cls_below, cls_above)[at],
            cy_send.at[at], cy_recv.at[at], sides[at][1],
        )

    def if_sent(at):
        return pl.when(sides[at][0] == 1)

    for at in range(2):
        @if_sent(2 + at)
        def _(at=at):
            for copy in x_copies(at):
                copy.start()

    @pl.loop(0, n - 1)
    def _(step):
        z_copy(step).start()

    for slot in (n, me):
        for at in range(2):
            @if_sent(at)
            def _(slot=slot, at=at):
                y_copy(slot, at).start()

    for at in range(2):
        @if_sent(3 - at)
        def _(at=at):
            for copy in x_copies(at):
                copy.wait_recv()

    for at, slot in enumerate((me, n)):
        merged = jnp.where(lane < 64, side_in[0, at].astype(F32), side_in[1, at].astype(F32))
        side[slot] = merged.astype(jnp.bfloat16)
    cls[:, tile_cols:wide] = jnp.where(lane < 64, cls_in[0], cls_in[1])

    for slot in (n, me):
        for at in range(2):
            @if_sent(at)
            def _(slot=slot, at=at):
                ys_copy(slot, at).start()

    for at in range(2):
        @if_sent(at)
        def _(at=at):
            cy_copy(at).start()

    @pl.loop(0, n - 1)
    def _(step):
        zs_copy(step).start()

    low_rows = lax.broadcasted_iota(jnp.int32, (2 * half, tile_cols), 0) % half < half // 2
    low_side = lax.broadcasted_iota(jnp.int32, (half, 128), 0) < half // 2
    lane_tall = lax.broadcasted_iota(jnp.int32, (tall, 128), 1) < 64

    def widened(slot, pair):
        head = core[slot, pair, 0].astype(F32)
        tail = core[slot, pair, 1].astype(F32)
        rim = jnp.where(low_rows, below[slot, pair].astype(F32), above[slot, pair].astype(F32))
        side_rim = jnp.where(
            low_side,
            side_below[slot].astype(F32)[0:half],
            side_above[slot].astype(F32)[half : 2 * half],
        )
        beside = jnp.concatenate([side[slot].astype(F32), side_rim], 0)
        both = []
        for at in range(2):
            low = SWEEPS * (2 * pair + at)
            cut = slice(at * half, (at + 1) * half)
            mine = jnp.concatenate([head[cut], tail[cut], rim[cut]], 0)
            end = jnp.where(
                lane_tall,
                pltpu.roll(beside, lax.rem(128 - low, 128), 1),
                pltpu.roll(beside, low, 1),
            )
            both.append(jnp.concatenate([mine, end], 1))
        return both

    def y_arrivals(slot):
        for at in range(2):
            @if_sent(1 - at)
            def _(at=at):
                y_copy(slot, at).wait_recv()
                ys_copy(slot, at).wait_recv()

    for at in range(2):
        @if_sent(1 - at)
        def _(at=at):
            cy_copy(at).wait_recv()

    low_cls = lax.broadcasted_iota(jnp.int32, (half, wide), 0) < half // 2
    kind = jnp.concatenate([cls[...], jnp.where(low_cls, cls_below[...], cls_above[...])], 0)
    picked = jnp.zeros((tall, wide), F32)
    for level in range(rates.shape[0]):
        picked = jnp.where(kind == level, rates[level], picked)
    rate[...] = picked
    keep[...] = 1.0 - 4.0 * picked

    y_arrivals(n)

    @pl.loop(0, pairs)
    def _(pair):
        for at, field in enumerate(widened(n, pair)):
            probe_field[2 * pair + at] = field * (1.0 / (n - 1))

    def add_member(slot, first):
        @pl.loop(0, pairs)
        def _(pair):
            for at, member in enumerate(widened(slot, pair)):
                slab = 2 * pair + at
                field = member * probe_field[slab]
                for _ in range(SWEEPS):
                    beside = (
                        pltpu.roll(field, 1, 0) + pltpu.roll(field, tall - 1, 0)
                        + pltpu.roll(field, 1, 1) + pltpu.roll(field, wide - 1, 1)
                    )
                    field = keep[...] * field + rate[...] * beside
                term = member[0:tile_rows, 0:tile_cols] * field[0:tile_rows, 0:tile_cols]
                out[slab] = term if first else out[slab] + term

    y_arrivals(me)
    add_member(me, True)

    @pl.loop(0, n - 1)
    def _(step):
        other = peer(step)
        z_arrival(other).wait_recv()
        for at in range(2):
            @if_sent(at)
            def _(at=at):
                y_copy(other, at).start()
        zs_arrival(other).wait_recv()
        for at in range(2):
            @if_sent(at)
            def _(at=at):
                ys_copy(other, at).start()
        y_arrivals(other)
        add_member(other, False)

    @pl.loop(0, n - 1)
    def _(step):
        z_copy(step).wait_send()
        zs_copy(step).wait_send()

    @pl.loop(0, n + 1)
    def _(slot):
        for at in range(2):
            @if_sent(at)
            def _(at=at):
                y_copy(slot, at).wait_send()
                ys_copy(slot, at).wait_send()

    for at in range(2):
        @if_sent(at)
        def _(at=at):
            cy_copy(at).wait_send()

        @if_sent(2 + at)
        def _(at=at):
            for copy in x_copies(at):
                copy.wait_send()


def body(n, rows, cols, pert, probes, diff_class, class_rate):
    mem_local, variables, levels, tile_rows, tile_cols = pert.shape
    slabs = variables * levels
    pairs = slabs // 2
    half = tile_rows // 2
    wide = tile_cols + 128
    tall = tile_rows + half
    bf16 = jnp.bfloat16
    flat = (slabs, tile_rows, tile_cols)
    vmem = pl.BlockSpec(memory_space=pltpu.VMEM)
    dma = pltpu.SemaphoreType.DMA
    out = pl.pallas_call(
        functools.partial(kernel, n, rows, cols),
        out_shape=jax.ShapeDtypeStruct(flat, F32),
        in_specs=[vmem, vmem, vmem, pl.BlockSpec(memory_space=pltpu.SMEM)],
        out_specs=vmem,
        scratch_shapes=[
            pltpu.VMEM((n + 1, pairs, 2, tile_rows, tile_cols), bf16),
            pltpu.VMEM((n + 1, pairs, tile_rows, tile_cols), bf16),
            pltpu.VMEM((n + 1, pairs, tile_rows, tile_cols), bf16),
            pltpu.VMEM((n + 1, tile_rows, 128), bf16),
            pltpu.VMEM((n + 1, tile_rows, 128), bf16),
            pltpu.VMEM((n + 1, tile_rows, 128), bf16),
            pltpu.VMEM((2, 2, tile_rows, 128), bf16),
            pltpu.VMEM((2, 2, tile_rows, 128), bf16),
            pltpu.VMEM((tile_rows, wide), jnp.int32),
            pltpu.VMEM((2, tile_rows, 128), jnp.int32),
            pltpu.VMEM((half, wide), jnp.int32),
            pltpu.VMEM((half, wide), jnp.int32),
            pltpu.VMEM((slabs, tall, wide), F32),
            pltpu.VMEM((tall, wide), F32),
            pltpu.VMEM((tall, wide), F32),
            dma((n,)), dma((n,)), dma((n,)), dma((n,)),
            dma((n + 1, 2)), dma((n + 1, 2)), dma((n + 1, 2)), dma((n + 1, 2)),
            dma((2,)), dma((2,)), dma((2,)), dma((2,)), dma((2,)), dma((2,)),
        ],
        compiler_params=pltpu.CompilerParams(
            collective_id=0, has_side_effects=True, vmem_limit_bytes=48 * 1024 * 1024
        ),
    )(pert.reshape(flat), probes.reshape(flat), diff_class, class_rate)
    return out.reshape(pert.shape)


def solution(mesh):
    placed = (
        P("member", None, None, "row", "col"),
        P("member", None, None, "row", "col"),
        P("row", "col"),
        P(),
    )
    sizes = (mesh.shape["member"], mesh.shape["row"], mesh.shape["col"])
    return jax.shard_map(
        functools.partial(body, *sizes),
        mesh=mesh,
        in_specs=placed,
        out_specs=P("member", None, None, "row", "col"),
        check_vma=False,
    )
```

time: 58.6 us -> 29.9 us (0.51)
  Pallas kernels: 0 us -> 25.7 us
  starting transfers between devices: 20.6 us -> 0 us
  blocking collectives: 19.2 us -> 0 us
  other arithmetic: 8.38 us -> 0 us
  waiting for transfers between devices: 7.39 us -> 0 us
  local copies, waits for them, and re-layouts: 2.43 us -> 3.88 us
    pallas_call x0 -> x1, Pallas kernels: none -> 25.7 us  [body(): pl.pallas_call(functools.partial(kernel, n, rows, cols), out_shape=jax.Sh...]
    ppermute x8 -> x0, starting transfers between devices: 20.6 us -> none  [the longest x4 15.5 us: extended(): lax.ppermute(tail, axis, [(i, (i + 1) % count) for i in range(ends)])]
    all_gather x1 -> x0, blocking collectives: 19.2 us -> none  [body(): member_piece = lax.all_gather(pert_wide, 'member', axis=0, tiled=True)]
    ppermute x8 -> x0, waiting for transfers between devices: 7.39 us -> none  [the longest x4 7.1 us: extended(): lax.ppermute(head, axis, [((i + 1) % count, i) for i in range(ends)])]
    mul x5 -> x0, other arithmetic: 4.92 us -> none  [the longest x3 4.78 us: deep_diffuse(): field_now = local_mask * (center + local_rate * (beside_all - 4.0 * center))]
    unnamed x1 -> x9, local copies, waits for them, and re-layouts: 0.9 us -> 3.88 us
    reduce_sum x2 -> x0, other arithmetic: 1.97 us -> none  [the longest x1 1.05 us: body(): jnp.sum(center_part[:, None].astype(jnp.float32) * field_now, axis=0)]
    concatenate x1 -> x0, local copies, waits for them, and re-layouts: 0.9 us -> none  [body(): stacked = jnp.concatenate([pert, probes], axis=0)]
  transfers between devices with their start and end apart: 8 -> 0, of which waited for: 3 -> 0; matrix products, arithmetic and copies ran while one was open for 3% -> 0% of each run, Pallas kernels for 0% -> 0%
where the time goes in v1:
time: 29.9 us; the launch traced here: 29.6 us
  Pallas kernels  25.7 us (86%)
  local copies, waits for them, and re-layouts  3.88 us (13%)
    pallas_call x1, Pallas kernels, body(): pl.pallas_call(functools.partial(kernel, n, rows, cols), out_shape=jax.Sh...  25.7 us
    unnamed x9, local copies, waits for them, and re-layouts  3.88 us

profile of v1, /device:TPU:0, one launch (start us, length us, event | category | flops | bytes accessed | tf_op | source)
XLA Modules:
  0.0 29.6 jit_solution(1125781648294751867)
XLA Ops:
  0.0 0.0 copy-start.3
  0.0 0.7 %copy-done.3 = f32[8]{0:T(128)S(1)} copy-done((f32[8]{0:T(128)S(1)}, f32[8]{0:T(128)}, u32[]{:S(2)}) %copy-start.3) | copy-done | bytes 56
  0.7 0.0 copy-start
  0.7 0.9 %copy-done = bf16[1,3,2,16,512]{4,3,2,1,0:T(8,128)(2,1)S(1)} copy-done((bf16[1,3,2,16,512]{4,3,2,1,0:T(8,128)(2,1)S(1)}, bf16[1,3,2,16,512]{4,3,2,1,0:T(8,128)(2,1)}, u32[]{:S(2)}) %copy-start) | copy-done | bytes 98328
  1.5 0.0 copy-start.1
  1.6 0.9 %copy-done.1 = bf16[1,3,2,16,512]{4,3,2,1,0:T(8,128)(2,1)S(1)} copy-done((bf16[1,3,2,16,512]{4,3,2,1,0:T(8,128)(2,1)S(1)}, bf16[1,3,2,16,512]{4,3,2,1,0:T(8,128)(2,1)}, u32[]{:S(2)}) %copy-start.1) | copy-done | bytes 98328
  2.4 0.0 copy-start.2
  2.4 0.8 %copy-done.2 = s32[16,512]{1,0:T(8,128)S(1)} copy-done((s32[16,512]{1,0:T(8,128)S(1)}, s32[16,512]{1,0:T(8,128)}, u32[]{:S(2)}) %copy-start.2) | copy-done | bytes 32792
  3.2 25.7 %shard_map.46 = f32[6,16,512]{2,1,0:T(8,128)S(1)} custom-call(bf16[6,16,512]{2,1,0:T(8,128)(2,1)S(1)} %bitcast.4, bf16[6,16,512]{2,1,0:T(8,128)(2,1)S(1)} %bitcast.5, s32[16,512]{1,0:T(8,128)S(1)} %copy-done.2, f32[8]{0:T(128)S(1)} %copy-done.3), custom_call_target="tpu_custom_call" | custom-call | tf_op jit(solution)/shard_map/pallas_call | solution.py:321
  29.0 0.7 %copy.6 = f32[1,3,2,16,512]{4,3,2,1,0:T(8,128)} copy(f32[1,3,2,16,512]{4,3,2,1,0:T(8,128)S(1)} %bitcast.3) | data formatting | bytes 393216
Async XLA Ops:
  0.0 0.7 %copy-start.3 = (f32[8]{0:T(128)S(1)}, f32[8]{0:T(128)}, u32[]{:S(2)}) copy-start(f32[8]{0:T(128)} %rates.1) | copy-start | bytes 100
  0.7 0.9 %copy-start = (bf16[1,3,2,16,512]{4,3,2,1,0:T(8,128)(2,1)S(1)}, bf16[1,3,2,16,512]{4,3,2,1,0:T(8,128)(2,1)}, u32[]{:S(2)}) copy-start(bf16[1,3,2,16,512]{4,3,2,1,0:T(8,128)(2,1)} %param.4) | copy-start | bytes 294916
  1.5 0.9 %copy-start.1 = (bf16[1,3,2,16,512]{4,3,2,1,0:T(8,128)(2,1)S(1)}, bf16[1,3,2,16,512]{4,3,2,1,0:T(8,128)(2,1)}, u32[]{:S(2)}) copy-start(bf16[1,3,2,16,512]{4,3,2,1,0:T(8,128)(2,1)} %param.5) | copy-start | bytes 294916
  2.4 0.8 %copy-start.2 = (s32[16,512]{1,0:T(8,128)S(1)}, s32[16,512]{1,0:T(8,128)}, u32[]{:S(2)}) copy-start(s32[16,512]{1,0:T(8,128)} %classes.1) | copy-start | bytes 98308

commit v2 on v1

--- a/solution.py
+++ b/solution.py
@@ -14,11 +14,12 @@
 
 def kernel(
     n, rows, cols,
-    pert, probes, classes, rates, out,
+    pert_hbm, probes_hbm, classes_hbm, rates_hbm, out,
+    pert, probes, classes, rates,
     core, above, below, side, side_above, side_below,
     side_out, side_in, cls, cls_in, cls_above, cls_below,
     probe_field, keep, rate,
-    z_send, z_recv, zs_send, zs_recv, y_send, y_recv, ys_send, ys_recv,
+    in_sem, z_send, z_recv, zs_send, zs_recv, y_send, y_recv, ys_send, ys_recv,
     x_send, x_recv, cx_send, cx_recv, cy_send, cy_recv,
 ):
     slabs, tile_rows, tile_cols = pert.shape
@@ -29,30 +30,32 @@
     me = lax.axis_index("member")
     row = lax.axis_index("row")
     col = lax.axis_index("col")
-    upper = (2 * me) // n
-
-    def peer(step):
-        mine = upper * (n - 1) + (1 - 2 * upper) * me
-        other = step + (step + n - mine) // n
-        return upper * (n - 1) + (1 - 2 * upper) * other
+
+    loads = [
+        pltpu.make_async_copy(src, dst, in_sem.at[at])
+        for at, (src, dst) in enumerate(
+            ((pert_hbm, pert), (probes_hbm, probes), (classes_hbm, classes), (rates_hbm, rates))
+        )
+    ]
+    for load in loads:
+        load.start()
 
     has_up = (row + rows - 1) // rows
     has_down = 1 - (row + 1) // rows
     has_left = (col + cols - 1) // cols
     has_right = 1 - (col + 1) // cols
+    has_prev = (me + n - 1) // n
+    has_next = 1 - (me + 1) // n
     sides = (
         (has_up, {"row": row - 1}),
         (has_down, {"row": row + 1}),
         (has_left, {"col": col - 1}),
         (has_right, {"col": col + 1}),
+        (has_prev, {"member": me - 1}),
+        (has_next, {"member": me + 1}),
     )
 
     barrier = pltpu.get_barrier_semaphore()
-
-    @pl.loop(0, n - 1)
-    def _(step):
-        pl.semaphore_signal(barrier, inc=1, device_id={"member": peer(step)}, device_id_type=MESH)
-
     for has, where in sides:
         @pl.when(has == 1)
         def _(where=where):
@@ -64,7 +67,8 @@
             device_id=where, device_id_type=MESH,
         )
 
-    for which, slot in ((pert, me), (probes, n)):
+    for load, which, slot in ((loads[0], pert, me), (loads[1], probes, n)):
+        load.wait()
         for pair in range(pairs):
             first = which[2 * pair].astype(F32)
             second = which[2 * pair + 1].astype(F32)
@@ -86,6 +90,8 @@
             to_right = jnp.where((lane >= 128 - SWEEPS - low) & (lane < 128 - low), tail, to_right)
         side_out[0, at] = to_left.astype(jnp.bfloat16)
         side_out[1, at] = to_right.astype(jnp.bfloat16)
+    loads[2].wait()
+    loads[3].wait()
     cls[:, 0:tile_cols] = classes[...]
 
     @pl.when(has_up == 0)
@@ -110,7 +116,7 @@
         side_in[1] = jnp.zeros_like(side_in[1])
         cls_in[1] = jnp.full_like(cls_in[1], -1)
 
-    pl.semaphore_wait(barrier, n - 1 + has_up + has_down + has_left + has_right)
+    pl.semaphore_wait(barrier, has_up + has_down + has_left + has_right + has_prev + has_next)
 
     def x_copies(at):
         where = sides[2 + at][1]
@@ -120,22 +126,21 @@
             remote(classes.at[:, block : block + 128], cls_in.at[at], cx_send.at[at], cx_recv.at[at], where),
         )
 
-    def z_copy(step):
-        return remote(core.at[me], core.at[me], z_send.at[step], z_recv.at[me], {"member": peer(step)})
-
-    def z_arrival(other):
-        return remote(core.at[other], core.at[other], z_send.at[0], z_recv.at[other], {"member": other})
-
-    def zs_copy(step):
-        return remote(side.at[me], side.at[me], zs_send.at[step], zs_recv.at[me], {"member": peer(step)})
-
-    def zs_arrival(other):
-        return remote(side.at[other], side.at[other], zs_send.at[0], zs_recv.at[other], {"member": other})
-
-    def y_copy(slot, at):
+    def z_copy(slot, pair, at):
         return remote(
-            core.at[slot, :, at], (below, above)[at].at[slot],
-            y_send.at[slot, at], y_recv.at[slot, at], sides[at][1],
+            core.at[slot, pair], core.at[slot, pair],
+            z_send.at[slot, pair, at], z_recv.at[slot, pair], sides[4 + at][1],
+        )
+
+    def zs_copy(slot, at):
+        return remote(
+            side.at[slot], side.at[slot], zs_send.at[slot, at], zs_recv.at[slot], sides[4 + at][1]
+        )
+
+    def y_copy(slot, pair, at):
+        return remote(
+            core.at[slot, pair, at], (below, above)[at].at[slot, pair],
+            y_send.at[slot, pair, at], y_recv.at[slot, pair, at], sides[at][1],
         )
 
     def ys_copy(slot, at):
@@ -159,15 +164,18 @@
             for copy in x_copies(at):
                 copy.start()
 
-    @pl.loop(0, n - 1)
-    def _(step):
-        z_copy(step).start()
+    for pair in range(pairs):
+        for at in range(2):
+            @if_sent(4 + at)
+            def _(pair=pair, at=at):
+                z_copy(me, pair, at).start()
 
     for slot in (n, me):
-        for at in range(2):
-            @if_sent(at)
-            def _(slot=slot, at=at):
-                y_copy(slot, at).start()
+        for pair in range(pairs):
+            for at in range(2):
+                @if_sent(at)
+                def _(slot=slot, pair=pair, at=at):
+                    y_copy(slot, pair, at).start()
 
     for at in range(2):
         @if_sent(3 - at)
@@ -191,9 +199,10 @@
         def _(at=at):
             cy_copy(at).start()
 
-    @pl.loop(0, n - 1)
-    def _(step):
-        zs_copy(step).start()
+    for at in range(2):
+        @if_sent(4 + at)
+        def _(at=at):
+            zs_copy(me, at).start()
 
     low_rows = lax.broadcasted_iota(jnp.int32, (2 * half, tile_cols), 0) % half < half // 2
     low_side = lax.broadcasted_iota(jnp.int32, (half, 128), 0) < half // 2
@@ -222,11 +231,16 @@
             both.append(jnp.concatenate([mine, end], 1))
         return both
 
-    def y_arrivals(slot):
+    def y_arrival(slot, pair):
         for at in range(2):
             @if_sent(1 - at)
             def _(at=at):
-                y_copy(slot, at).wait_recv()
+                y_copy(slot, pair, at).wait_recv()
+
+    def ys_arrival(slot):
+        for at in range(2):
+            @if_sent(1 - at)
+            def _(at=at):
                 ys_copy(slot, at).wait_recv()
 
     for at in range(2):
@@ -242,58 +256,97 @@
     rate[...] = picked
     keep[...] = 1.0 - 4.0 * picked
 
-    y_arrivals(n)
+    ys_arrival(n)
 
     @pl.loop(0, pairs)
     def _(pair):
+        y_arrival(n, pair)
         for at, field in enumerate(widened(n, pair)):
             probe_field[2 * pair + at] = field * (1.0 / (n - 1))
-
-    def add_member(slot, first):
+            out[2 * pair + at] = jnp.zeros((tile_rows, tile_cols), F32)
+
+    def add_pair(slot, pair):
+        y_arrival(slot, pair)
+        for at, member in enumerate(widened(slot, pair)):
+            slab = 2 * pair + at
+            field = member * probe_field[slab]
+            for _ in range(SWEEPS):
+                beside = (
+                    pltpu.roll(field, 1, 0) + pltpu.roll(field, tall - 1, 0)
+                    + pltpu.roll(field, 1, 1) + pltpu.roll(field, wide - 1, 1)
+                )
+                field = keep[...] * field + rate[...] * beside
+            out[slab] += member[0:tile_rows, 0:tile_cols] * field[0:tile_rows, 0:tile_cols]
+
+    def hand_on(slot, pair, onward):
+        z_copy(slot, pair, onward).wait_recv()
+
+        @if_sent(4 + onward)
+        def _():
+            z_copy(slot, pair, onward).start()
+
+        for at in range(2):
+            @if_sent(at)
+            def _(at=at):
+                y_copy(slot, pair, at).start()
+
+    def hand_on_side(slot, onward):
+        zs_copy(slot, onward).wait_recv()
+
+        @if_sent(4 + onward)
+        def _():
+            zs_copy(slot, onward).start()
+
+        for at in range(2):
+            @if_sent(at)
+            def _(at=at):
+                ys_copy(slot, at).start()
+
+    def at_distance(away, act):
+        @pl.when(me - away >= 0)
+        def _():
+            act(me - away, 1)
+
+        @pl.when(me + away < n)
+        def _():
+            act(me + away, 0)
+
+    ys_arrival(me)
+
+    @pl.loop(0, pairs)
+    def _(pair):
+        at_distance(1, lambda slot, onward: hand_on(slot, pair, onward))
+        add_pair(me, pair)
+
+    at_distance(1, hand_on_side)
+
+    @pl.loop(1, n)
+    def _(away):
+        at_distance(away, lambda slot, onward: ys_arrival(slot))
+
         @pl.loop(0, pairs)
         def _(pair):
-            for at, member in enumerate(widened(slot, pair)):
-                slab = 2 * pair + at
-                field = member * probe_field[slab]
-                for _ in range(SWEEPS):
-                    beside = (
-                        pltpu.roll(field, 1, 0) + pltpu.roll(field, tall - 1, 0)
-                        + pltpu.roll(field, 1, 1) + pltpu.roll(field, wide - 1, 1)
-                    )
-                    field = keep[...] * field + rate[...] * beside
-                term = member[0:tile_rows, 0:tile_cols] * field[0:tile_rows, 0:tile_cols]
-                out[slab] = term if first else out[slab] + term
-
-    y_arrivals(me)
-    add_member(me, True)
-
-    @pl.loop(0, n - 1)
-    def _(step):
-        other = peer(step)
-        z_arrival(other).wait_recv()
-        for at in range(2):
-            @if_sent(at)
-            def _(at=at):
-                y_copy(other, at).start()
-        zs_arrival(other).wait_recv()
-        for at in range(2):
-            @if_sent(at)
-            def _(at=at):
-                ys_copy(other, at).start()
-        y_arrivals(other)
-        add_member(other, False)
-
-    @pl.loop(0, n - 1)
-    def _(step):
-        z_copy(step).wait_send()
-        zs_copy(step).wait_send()
+            at_distance(away + 1, lambda slot, onward: hand_on(slot, pair, onward))
+            at_distance(away, lambda slot, onward: add_pair(slot, pair))
+
+        at_distance(away + 1, hand_on_side)
+
+    @pl.loop(0, n)
+    def _(slot):
+        for at in range(2):
+            @pl.when((sides[4 + at][0] == 1) & ((slot >= me) if at == 0 else (slot <= me)))
+            def _(at=at):
+                for pair in range(pairs):
+                    z_copy(slot, pair, at).wait_send()
+                zs_copy(slot, at).wait_send()
 
     @pl.loop(0, n + 1)
     def _(slot):
         for at in range(2):
             @if_sent(at)
             def _(at=at):
-                y_copy(slot, at).wait_send()
+                for pair in range(pairs):
+                    y_copy(slot, pair, at).wait_send()
                 ys_copy(slot, at).wait_send()
 
     for at in range(2):
@@ -321,9 +374,13 @@
     out = pl.pallas_call(
         functools.partial(kernel, n, rows, cols),
         out_shape=jax.ShapeDtypeStruct(flat, F32),
-        in_specs=[vmem, vmem, vmem, pl.BlockSpec(memory_space=pltpu.SMEM)],
+        in_specs=[pl.BlockSpec(memory_space=pltpu.HBM)] * 4,
         out_specs=vmem,
         scratch_shapes=[
+            pltpu.VMEM(flat, bf16),
+            pltpu.VMEM(flat, bf16),
+            pltpu.VMEM((tile_rows, tile_cols), jnp.int32),
+            pltpu.SMEM(class_rate.shape, F32),
             pltpu.VMEM((n + 1, pairs, 2, tile_rows, tile_cols), bf16),
             pltpu.VMEM((n + 1, pairs, tile_rows, tile_cols), bf16),
             pltpu.VMEM((n + 1, pairs, tile_rows, tile_cols), bf16),
@@ -339,12 +396,12 @@
             pltpu.VMEM((slabs, tall, wide), F32),
             pltpu.VMEM((tall, wide), F32),
             pltpu.VMEM((tall, wide), F32),
-            dma((n,)), dma((n,)), dma((n,)), dma((n,)),
-            dma((n + 1, 2)), dma((n + 1, 2)), dma((n + 1, 2)), dma((n + 1, 2)),
+            dma((4,)), dma((n, pairs, 2)), dma((n, pairs)), dma((n, 2)), dma((n,)),
+            dma((n + 1, pairs, 2)), dma((n + 1, pairs, 2)), dma((n + 1, 2)), dma((n + 1, 2)),
             dma((2,)), dma((2,)), dma((2,)), dma((2,)), dma((2,)), dma((2,)),
         ],
         compiler_params=pltpu.CompilerParams(
-            collective_id=0, has_side_effects=True, vmem_limit_bytes=48 * 1024 * 1024
+            collective_id=0, has_side_effects=True, vmem_limit_bytes=64 * 1024 * 1024
         ),
     )(pert.reshape(flat), probes.reshape(flat), diff_class, class_rate)
     return out.reshape(pert.shape)

time: 29.9 us -> 27.6 us (0.923)
  the two profiles are of different devices: /device:TPU:0 before, /device:TPU:1 now
where the time goes in v2:
time: 27.6 us; the launch traced here: 27.4 us
  Pallas kernels  25.8 us (93%)
  local copies, waits for them, and re-layouts  1.62 us (6%)
    pallas_call x1, Pallas kernels, body(): pl.pallas_call(functools.partial(kernel, n, rows, cols), out_shape=jax.Sh...  25.8 us
    unnamed x1, local copies, waits for them, and re-layouts  1.62 us

profile of v2, /device:TPU:1, one launch (start us, length us, event | category | flops | bytes accessed | tf_op | source)
XLA Modules:
  0.0 27.4 jit_solution(16040806073407102099)
XLA Ops:
  0.0 25.8 %shard_map.46 = f32[6,16,512]{2,1,0:T(8,128)} custom-call(bf16[6,16,512]{2,1,0:T(8,128)(2,1)} %bitcast.4, bf16[6,16,512]{2,1,0:T(8,128)(2,1)} %bitcast.5, s32[16,512]{1,0:T(8,128)} %classes_hbm.1, f32[8]{0:T(128)} %rates_hbm.1), custom_call_target="tpu_custom_call" | custom-call | tf_op jit(solution)/shard_map/pallas_call | solution.py:374
  25.8 1.6 %copy.6 = f32[1,3,2,16,512]{4,3,2,1,0:T(8,128)} copy(f32[1,3,2,16,512]{4,3,2,1,0:T(8,128)} %bitcast.3) | data formatting | bytes 393216

commit v3 on v2

--- a/solution.py
+++ b/solution.py
@@ -8,6 +8,7 @@
 from jax.sharding import PartitionSpec as P
 
 SWEEPS = 4
+SUBLANES = 8
 MESH = pl.DeviceIdType.MESH
 F32 = jnp.float32
 
@@ -18,7 +19,7 @@
     pert, probes, classes, rates,
     core, above, below, side, side_above, side_below,
     side_out, side_in, cls, cls_in, cls_above, cls_below,
-    probe_field, keep, rate,
+    probe_field, keep, rate, turned, field_a, field_b, result,
     in_sem, z_send, z_recv, zs_send, zs_recv, y_send, y_recv, ys_send, ys_recv,
     x_send, x_recv, cx_send, cx_recv, cy_send, cy_recv,
 ):
@@ -253,8 +254,10 @@
     picked = jnp.zeros((tall, wide), F32)
     for level in range(rates.shape[0]):
         picked = jnp.where(kind == level, rates[level], picked)
-    rate[...] = picked
-    keep[...] = 1.0 - 4.0 * picked
+    for at in range(tall):
+        line = jnp.broadcast_to(picked[at : at + 1], (SUBLANES, wide))
+        rate[at] = line
+        keep[at] = 1.0 - 4.0 * line
 
     ys_arrival(n)
 
@@ -262,21 +265,68 @@
     def _(pair):
         y_arrival(n, pair)
         for at, field in enumerate(widened(n, pair)):
-            probe_field[2 * pair + at] = field * (1.0 / (n - 1))
+            probe_field[2 * pair + at] = field
             out[2 * pair + at] = jnp.zeros((tile_rows, tile_cols), F32)
 
-    def add_pair(slot, pair):
-        y_arrival(slot, pair)
-        for at, member in enumerate(widened(slot, pair)):
-            slab = 2 * pair + at
-            field = member * probe_field[slab]
-            for _ in range(SWEEPS):
-                beside = (
-                    pltpu.roll(field, 1, 0) + pltpu.roll(field, tall - 1, 0)
-                    + pltpu.roll(field, 1, 1) + pltpu.roll(field, wide - 1, 1)
+    blocks = wide // 128
+    if slabs < SUBLANES:
+        turned[:, slabs * tall :] = jnp.zeros((blocks, (SUBLANES - slabs) * tall, 128), F32)
+
+    def sweep(load, store, margin):
+        above_now, now = load(-margin - 1), load(-margin)
+        for at in range(-margin, tile_rows + margin):
+            below_now = load(at + 1)
+            beside = above_now + below_now + pltpu.roll(now, 1, 1) + pltpu.roll(now, wide - 1, 1)
+            store(at, keep[at % tall] * now + rate[at % tall] * beside)
+            above_now, now = now, below_now
+
+    def load_turned(at):
+        picks = [
+            turned[block, pl.ds(at % tall, SUBLANES, stride=tall), :] for block in range(blocks)
+        ]
+        return jnp.concatenate(picks, 1)
+
+    def store_result(at, value):
+        for block in range(tile_cols // 128):
+            result[block, pl.ds(at, SUBLANES, stride=tile_rows), :] = value[:, block * 128 : (block + 1) * 128]
+
+    def through(buffer):
+        def load(at):
+            return buffer[at % tall]
+
+        def store(at, value):
+            buffer[at % tall] = value
+
+        return load, store
+
+    def add_member(slot):
+        for pair in range(pairs):
+            y_arrival(slot, pair)
+        ys_arrival(slot)
+        for pair in range(pairs):
+            for at, member in enumerate(widened(slot, pair)):
+                slab = 2 * pair + at
+                field = member * probe_field[slab]
+                for block in range(blocks):
+                    turned[block, slab * tall : (slab + 1) * tall] = field[:, block * 128 : (block + 1) * 128]
+        load_a, store_a = through(field_a)
+        load_b, store_b = through(field_b)
+        loads_now = load_turned
+        for step in range(SWEEPS):
+            store_now = store_result if step == SWEEPS - 1 else (store_a, store_b)[step % 2]
+            sweep(loads_now, store_now, SWEEPS - 1 - step)
+            loads_now = (load_a, load_b)[step % 2]
+        for pair in range(pairs):
+            head = core[slot, pair, 0].astype(F32)
+            tail = core[slot, pair, 1].astype(F32)
+            for at in range(2):
+                slab = 2 * pair + at
+                cut = slice(at * half, (at + 1) * half)
+                member = jnp.concatenate([head[cut], tail[cut]], 0)
+                done = jnp.concatenate(
+                    [result[block, slab * tile_rows : (slab + 1) * tile_rows] for block in range(tile_cols // 128)], 1
                 )
-                field = keep[...] * field + rate[...] * beside
-            out[slab] += member[0:tile_rows, 0:tile_cols] * field[0:tile_rows, 0:tile_cols]
+                out[slab] += member * done
 
     def hand_on(slot, pair, onward):
         z_copy(slot, pair, onward).wait_recv()
@@ -311,25 +361,19 @@
         def _():
             act(me + away, 0)
 
-    ys_arrival(me)
-
-    @pl.loop(0, pairs)
-    def _(pair):
-        at_distance(1, lambda slot, onward: hand_on(slot, pair, onward))
-        add_pair(me, pair)
-
-    at_distance(1, hand_on_side)
+    def around(away, work):
+        early = pairs - 1
+        for pair in range(early):
+            at_distance(away, lambda slot, onward: hand_on(slot, pair, onward))
+        work()
+        at_distance(away, lambda slot, onward: hand_on(slot, early, onward))
+        at_distance(away, hand_on_side)
+
+    around(1, lambda: add_member(me))
 
     @pl.loop(1, n)
     def _(away):
-        at_distance(away, lambda slot, onward: ys_arrival(slot))
-
-        @pl.loop(0, pairs)
-        def _(pair):
-            at_distance(away + 1, lambda slot, onward: hand_on(slot, pair, onward))
-            at_distance(away, lambda slot, onward: add_pair(slot, pair))
-
-        at_distance(away + 1, hand_on_side)
+        around(away + 1, lambda: at_distance(away, lambda slot, onward: add_member(slot)))
 
     @pl.loop(0, n)
     def _(slot):
@@ -394,8 +438,12 @@
             pltpu.VMEM((half, wide), jnp.int32),
             pltpu.VMEM((half, wide), jnp.int32),
             pltpu.VMEM((slabs, tall, wide), F32),
-            pltpu.VMEM((tall, wide), F32),
-            pltpu.VMEM((tall, wide), F32),
+            pltpu.VMEM((tall, SUBLANES, wide), F32),
+            pltpu.VMEM((tall, SUBLANES, wide), F32),
+            pltpu.VMEM((wide // 128, SUBLANES * tall, 128), F32),
+            pltpu.VMEM((tall, SUBLANES, wide), F32),
+            pltpu.VMEM((tall, SUBLANES, wide), F32),
+            pltpu.VMEM((tile_cols // 128, SUBLANES * tile_rows, 128), F32),
             dma((4,)), dma((n, pairs, 2)), dma((n, pairs)), dma((n, 2)), dma((n,)),
             dma((n + 1, pairs, 2)), dma((n + 1, pairs, 2)), dma((n + 1, 2)), dma((n + 1, 2)),
             dma((2,)), dma((2,)), dma((2,)), dma((2,)), dma((2,)), dma((2,)),
@@ -404,7 +452,7 @@
             collective_id=0, has_side_effects=True, vmem_limit_bytes=64 * 1024 * 1024
         ),
     )(pert.reshape(flat), probes.reshape(flat), diff_class, class_rate)
-    return out.reshape(pert.shape)
+    return out.reshape(pert.shape) / (n - 1)
 
 
 def solution(mesh):

time: 27.6 us -> 25.7 us (0.931)
  Pallas kernels: 25.8 us -> 24 us
  other arithmetic: 0 us -> 1.62 us
  local copies, waits for them, and re-layouts: 1.62 us -> 0 us
    pallas_call x1, Pallas kernels: 25.8 us -> 24 us  [body(): pl.pallas_call(functools.partial(kernel, n, rows, cols), out_shape=jax.Sh...]
    div x0 -> x1, other arithmetic: none -> 1.62 us  [body(): return out.reshape(pert.shape) / (n - 1)]
    unnamed x1 -> x0, local copies, waits for them, and re-layouts: 1.62 us -> none
where the time goes in v3:
time: 25.7 us; the launch traced here: 25.6 us
  Pallas kernels  24 us (93%)
  other arithmetic  1.62 us (6%)
    pallas_call x1, Pallas kernels, body(): pl.pallas_call(functools.partial(kernel, n, rows, cols), out_shape=jax.Sh...  24 us
    div x1, other arithmetic, body(): return out.reshape(pert.shape) / (n - 1)  1.62 us

profile of v3, /device:TPU:1, one launch (start us, length us, event | category | flops | bytes accessed | tf_op | source)
XLA Modules:
  0.0 25.6 jit_solution(10040556163997905524)
XLA Ops:
  0.0 24.0 %shard_map.46 = f32[6,16,512]{2,1,0:T(8,128)} custom-call(bf16[6,16,512]{2,1,0:T(8,128)(2,1)} %bitcast.3, bf16[6,16,512]{2,1,0:T(8,128)(2,1)} %bitcast.4, s32[16,512]{1,0:T(8,128)} %classes_hbm.1, f32[8]{0:T(128)} %rates_hbm.1), custom_call_target="tpu_custom_call" | custom-call | tf_op jit(solution)/shard_map/pallas_call | solution.py:418
  24.0 1.6 %broadcast_multiply_fusion = f32[6,16,512]{2,1,0:T(8,128)} fusion(f32[6,16,512]{2,1,0:T(8,128)} %shard_map.46), kind=kLoop, calls=%fused_computation | loop fusion | flops 49152 | bytes 393216 | tf_op jit(solution)/shard_map/div | solution.py:455

commit v4 on v3

--- a/solution.py
+++ b/solution.py
@@ -68,14 +68,73 @@
             device_id=where, device_id_type=MESH,
         )
 
-    for load, which, slot in ((loads[0], pert, me), (loads[1], probes, n)):
-        load.wait()
+    def x_copies(at):
+        where = sides[2 + at][1]
+        block = (0, tile_cols - 128)[at]
+        return (
+            remote(side_out.at[at], side_in.at[at], x_send.at[at], x_recv.at[at], where),
+            remote(classes.at[:, block : block + 128], cls_in.at[at], cx_send.at[at], cx_recv.at[at], where),
+        )
+
+    def z_copy(slot, pair, at):
+        return remote(
+            core.at[slot, pair], core.at[slot, pair],
+            z_send.at[slot, pair, at], z_recv.at[slot, pair], sides[4 + at][1],
+        )
+
+    def zs_copy(slot, at):
+        return remote(
+            side.at[slot], side.at[slot], zs_send.at[slot, at], zs_recv.at[slot], sides[4 + at][1]
+        )
+
+    def y_copy(slot, pair, at):
+        return remote(
+            core.at[slot, pair, at], (below, above)[at].at[slot, pair],
+            y_send.at[slot, pair, at], y_recv.at[slot, pair, at], sides[at][1],
+        )
+
+    def ys_copy(slot, at):
+        return remote(
+            side.at[slot], (side_below, side_above)[at].at[slot],
+            ys_send.at[slot, at], ys_recv.at[slot, at], sides[at][1],
+        )
+
+    def cy_copy(at):
+        return remote(
+            cls.at[at * half : (at + 1) * half], (cls_below, cls_above)[at],
+            cy_send.at[at], cy_recv.at[at], sides[at][1],
+        )
+
+    def if_sent(at):
+        return pl.when(sides[at][0] == 1)
+
+    def pack(which, slot):
         for pair in range(pairs):
             first = which[2 * pair].astype(F32)
             second = which[2 * pair + 1].astype(F32)
             for part in range(2):
                 cut = slice(part * half, (part + 1) * half)
                 core[slot, pair, part] = jnp.concatenate([first[cut], second[cut]], 0).astype(jnp.bfloat16)
+
+    def start_rows(slot):
+        for pair in range(pairs):
+            for at in range(2):
+                @if_sent(at)
+                def _(pair=pair, at=at):
+                    y_copy(slot, pair, at).start()
+
+    loads[0].wait()
+    pack(pert, me)
+    pl.semaphore_wait(barrier, has_up + has_down + has_left + has_right + has_prev + has_next)
+
+    for pair in range(pairs):
+        for at in range(2):
+            @if_sent(4 + at)
+            def _(pair=pair, at=at):
+                z_copy(me, pair, at).start()
+
+    for load in loads[1:]:
+        load.wait()
     lane = lax.broadcasted_iota(jnp.int32, (tile_rows, 128), 1)
     for at, which in enumerate((pert, probes)):
         to_left = jnp.zeros((tile_rows, 128), F32)
@@ -91,8 +150,15 @@
             to_right = jnp.where((lane >= 128 - SWEEPS - low) & (lane < 128 - low), tail, to_right)
         side_out[0, at] = to_left.astype(jnp.bfloat16)
         side_out[1, at] = to_right.astype(jnp.bfloat16)
-    loads[2].wait()
-    loads[3].wait()
+    for at in range(2):
+        @if_sent(2 + at)
+        def _(at=at):
+            for copy in x_copies(at):
+                copy.start()
+
+    pack(probes, n)
+    start_rows(n)
+    start_rows(me)
     cls[:, 0:tile_cols] = classes[...]
 
     @pl.when(has_up == 0)
@@ -116,67 +182,6 @@
     def _():
         side_in[1] = jnp.zeros_like(side_in[1])
         cls_in[1] = jnp.full_like(cls_in[1], -1)
-
-    pl.semaphore_wait(barrier, has_up + has_down + has_left + has_right + has_prev + has_next)
-
-    def x_copies(at):
-        where = sides[2 + at][1]
-        block = (0, tile_cols - 128)[at]
-        return (
-            remote(side_out.at[at], side_in.at[at], x_send.at[at], x_recv.at[at], where),
-            remote(classes.at[:, block : block + 128], cls_in.at[at], cx_send.at[at], cx_recv.at[at], where),
-        )
-
-    def z_copy(slot, pair, at):
-        return remote(
-            core.at[slot, pair], core.at[slot, pair],
-            z_send.at[slot, pair, at], z_recv.at[slot, pair], sides[4 + at][1],
-        )
-
-    def zs_copy(slot, at):
-        return remote(
-            side.at[slot], side.at[slot], zs_send.at[slot, at], zs_recv.at[slot], sides[4 + at][1]
-        )
-
-    def y_copy(slot, pair, at):
-        return remote(
-            core.at[slot, pair, at], (below, above)[at].at[slot, pair],
-            y_send.at[slot, pair, at], y_recv.at[slot, pair, at], sides[at][1],
-        )
-
-    def ys_copy(slot, at):
-        return remote(
-            side.at[slot], (side_below, side_above)[at].at[slot],
-            ys_send.at[slot, at], ys_recv.at[slot, at], sides[at][1],
-        )
-
-    def cy_copy(at):
-        return remote(
-            cls.at[at * half : (at + 1) * half], (cls_below, cls_above)[at],
-            cy_send.at[at], cy_recv.at[at], sides[at][1],
-        )
-
-    def if_sent(at):
-        return pl.when(sides[at][0] == 1)
-
-    for at in range(2):
-        @if_sent(2 + at)
-        def _(at=at):
-            for copy in x_copies(at):
-                copy.start()
-
-    for pair in range(pairs):
-        for at in range(2):
-            @if_sent(4 + at)
-            def _(pair=pair, at=at):
-                z_copy(me, pair, at).start()
-
-    for slot in (n, me):
-        for pair in range(pairs):
-            for at in range(2):
-                @if_sent(at)
-                def _(slot=slot, pair=pair, at=at):
-                    y_copy(slot, pair, at).start()
 
     for at in range(2):
         @if_sent(3 - at)
@@ -361,19 +366,26 @@
         def _():
             act(me + away, 0)
 
-    def around(away, work):
-        early = pairs - 1
-        for pair in range(early):
+    def arrivals(away):
+        for pair in range(pairs):
             at_distance(away, lambda slot, onward: hand_on(slot, pair, onward))
-        work()
-        at_distance(away, lambda slot, onward: hand_on(slot, early, onward))
         at_distance(away, hand_on_side)
 
-    around(1, lambda: add_member(me))
-
-    @pl.loop(1, n)
-    def _(away):
-        around(away + 1, lambda: at_distance(away, lambda slot, onward: add_member(slot)))
+    lower = 1 - (2 * me) // n
+
+    @pl.loop(0, 2 * n)
+    def _(turn):
+        away = turn // 2
+        second = turn % 2
+        slot = me + away * (2 * ((second + lower) % 2) - 1)
+
+        @pl.when(second == 1)
+        def _():
+            arrivals(away + 1)
+
+        @pl.when((slot >= 0) & (slot < n) & (turn > 0))
+        def _():
+            add_member(slot)
 
     @pl.loop(0, n)
     def _(slot):
@@ -417,7 +429,7 @@
     dma = pltpu.SemaphoreType.DMA
     out = pl.pallas_call(
         functools.partial(kernel, n, rows, cols),
-        out_shape=jax.ShapeDtypeStruct(flat, F32),
+        out_shape=pltpu.VMEM(flat, F32),
         in_specs=[pl.BlockSpec(memory_space=pltpu.HBM)] * 4,
         out_specs=vmem,
         scratch_shapes=[
@@ -449,7 +461,7 @@
             dma((2,)), dma((2,)), dma((2,)), dma((2,)), dma((2,)), dma((2,)),
         ],
         compiler_params=pltpu.CompilerParams(
-            collective_id=0, has_side_effects=True, vmem_limit_bytes=64 * 1024 * 1024
+            collective_id=0, has_side_effects=True, vmem_limit_bytes=60 * 1024 * 1024
         ),
     )(pert.reshape(flat), probes.reshape(flat), diff_class, class_rate)
     return out.reshape(pert.shape) / (n - 1)

time: 25.7 us -> 23.8 us (0.926)
  Pallas kernels: 24 us -> 23 us
  other arithmetic: 1.62 us -> 0.7 us
    pallas_call x1, Pallas kernels: 24 us -> 23 us  [body(): pl.pallas_call(functools.partial(kernel, n, rows, cols), out_shape=pltpu....]
    div x1, other arithmetic: 1.62 us -> 0.7 us  [body(): return out.reshape(pert.shape) / (n - 1)]
where the time goes in v4:
time: 23.8 us; the launch traced here: 23.7 us
  Pallas kernels  23 us (97%)
  other arithmetic  0.7 us (3%)
    pallas_call x1, Pallas kernels, body(): pl.pallas_call(functools.partial(kernel, n, rows, cols), out_shape=pltpu....  23 us
    div x1, other arithmetic, body(): return out.reshape(pert.shape) / (n - 1)  0.7 us

profile of v4, /device:TPU:1, one launch (start us, length us, event | category | flops | bytes accessed | tf_op | source)
XLA Modules:
  0.0 23.7 jit_solution(13419827900696205850)
XLA Ops:
  0.0 23.0 %shard_map.46 = f32[6,16,512]{2,1,0:T(8,128)S(1)} custom-call(bf16[6,16,512]{2,1,0:T(8,128)(2,1)} %bitcast.3, bf16[6,16,512]{2,1,0:T(8,128)(2,1)} %bitcast.4, s32[16,512]{1,0:T(8,128)} %classes_hbm.1, f32[8]{0:T(128)} %rates_hbm.1), custom_call_target="tpu_custom_call" | custom-call | tf_op jit(solution)/shard_map/pallas_call | solution.py:430
  23.0 0.7 %broadcast_multiply_fusion = f32[6,16,512]{2,1,0:T(8,128)} fusion(f32[6,16,512]{2,1,0:T(8,128)S(1)} %shard_map.46), kind=kLoop, calls=%fused_computation | loop fusion | flops 49152 | bytes 393216 | tf_op jit(solution)/shard_map/div | solution.py:467

commit v5 on v4

--- a/solution.py
+++ b/solution.py
@@ -19,7 +19,7 @@
     pert, probes, classes, rates,
     core, above, below, side, side_above, side_below,
     side_out, side_in, cls, cls_in, cls_above, cls_below,
-    probe_field, keep, rate, turned, field_a, field_b, result,
+    probe_field, keep, rate, turned, field_a, field_b, result, total,
     in_sem, z_send, z_recv, zs_send, zs_recv, y_send, y_recv, ys_send, ys_recv,
     x_send, x_recv, cx_send, cx_recv, cy_send, cy_recv,
 ):
@@ -108,13 +108,28 @@
     def if_sent(at):
         return pl.when(sides[at][0] == 1)
 
+    fold = tile_cols // 2
+    low_rows = lax.broadcasted_iota(jnp.int32, (half, tile_cols), 0) < half // 2
+    low_side = lax.broadcasted_iota(jnp.int32, (half, 128), 0) < half // 2
+
+    def swap(rows_now):
+        return pltpu.roll(rows_now, half // 2, 0)
+
+    def folded(rows_now):
+        return jnp.concatenate([rows_now[:, :fold], rows_now[:, fold:]], 0).astype(jnp.bfloat16)
+
+    def unfolded(block):
+        both = block.astype(F32)
+        return jnp.concatenate([both[:half], both[half:]], 1)
+
     def pack(which, slot):
         for pair in range(pairs):
             first = which[2 * pair].astype(F32)
             second = which[2 * pair + 1].astype(F32)
-            for part in range(2):
-                cut = slice(part * half, (part + 1) * half)
-                core[slot, pair, part] = jnp.concatenate([first[cut], second[cut]], 0).astype(jnp.bfloat16)
+            core[slot, pair, 0] = folded(jnp.where(low_rows, first[:half], swap(second[:half])))
+            core[slot, pair, 1] = folded(jnp.where(low_rows, swap(first[half:]), second[half:]))
+            for at, tile in enumerate((first, second)):
+                core[slot, pair, 2 + at] = folded(jnp.where(low_rows, swap(tile[:half]), swap(tile[half:])))
 
     def start_rows(slot):
         for pair in range(pairs):
@@ -148,8 +163,10 @@
                 tail = pltpu.roll(tail, 128 - low, 1)
             to_left = jnp.where((lane >= low) & (lane < low + SWEEPS), head, to_left)
             to_right = jnp.where((lane >= 128 - SWEEPS - low) & (lane < 128 - low), tail, to_right)
-        side_out[0, at] = to_left.astype(jnp.bfloat16)
-        side_out[1, at] = to_right.astype(jnp.bfloat16)
+        for way, rim in enumerate((to_left, to_right)):
+            ends = jnp.where(low_side, rim[:half], rim[half:])
+            middle = jnp.where(low_side, swap(rim[:half]), swap(rim[half:]))
+            side_out[way, at] = jnp.concatenate([ends, middle], 0).astype(jnp.bfloat16)
     for at in range(2):
         @if_sent(2 + at)
         def _(at=at):
@@ -210,32 +227,55 @@
         def _(at=at):
             zs_copy(me, at).start()
 
-    low_rows = lax.broadcasted_iota(jnp.int32, (2 * half, tile_cols), 0) % half < half // 2
-    low_side = lax.broadcasted_iota(jnp.int32, (half, 128), 0) < half // 2
     lane_tall = lax.broadcasted_iota(jnp.int32, (tall, 128), 1) < 64
 
+    def place(at):
+        return at + half if at < 0 else at if at < half // 2 else at + half // 2
+
     def widened(slot, pair):
-        head = core[slot, pair, 0].astype(F32)
-        tail = core[slot, pair, 1].astype(F32)
-        rim = jnp.where(low_rows, below[slot, pair].astype(F32), above[slot, pair].astype(F32))
-        side_rim = jnp.where(
-            low_side,
-            side_below[slot].astype(F32)[0:half],
-            side_above[slot].astype(F32)[half : 2 * half],
-        )
-        beside = jnp.concatenate([side[slot].astype(F32), side_rim], 0)
+        top, bottom = unfolded(core[slot, pair, 0]), unfolded(core[slot, pair, 1])
+        over, under = unfolded(above[slot, pair]), unfolded(below[slot, pair])
+        beside_own = side[slot].astype(F32)
+        ends, middle = beside_own[:half], beside_own[half:]
+        beside = jnp.concatenate(
+            [
+                jnp.where(low_side, ends, side_above[slot].astype(F32)[:half]),
+                middle,
+                swap(jnp.where(low_side, side_below[slot].astype(F32)[:half], ends)),
+            ],
+            0,
+        )
         both = []
         for at in range(2):
             low = SWEEPS * (2 * pair + at)
-            cut = slice(at * half, (at + 1) * half)
-            mine = jnp.concatenate([head[cut], tail[cut], rim[cut]], 0)
+            if at == 0:
+                head = jnp.where(low_rows, top, swap(over))
+                tail = jnp.where(low_rows, bottom, swap(under))
+            else:
+                head = jnp.where(low_rows, swap(top), over)
+                tail = jnp.where(low_rows, swap(bottom), under)
+            mine = jnp.concatenate([head, unfolded(core[slot, pair, 2 + at]), tail], 0)
             end = jnp.where(
                 lane_tall,
-                pltpu.roll(beside, lax.rem(128 - low, 128), 1),
-                pltpu.roll(beside, low, 1),
+                pltpu.roll(beside, (128 - low) % 128, 1) if low else beside,
+                pltpu.roll(beside, low, 1) if low else beside,
             )
             both.append(jnp.concatenate([mine, end], 1))
         return both
+
+    def centre(slot, pair):
+        top, bottom = unfolded(core[slot, pair, 0]), unfolded(core[slot, pair, 1])
+        return [
+            jnp.concatenate([ends, unfolded(core[slot, pair, 2 + at])], 0)
+            for at, ends in enumerate(
+                (jnp.where(low_rows, top, swap(bottom)), jnp.where(low_rows, swap(top), bottom))
+            )
+        ]
+
+    def result_place(at):
+        if at < half // 2:
+            return at
+        return at - half if at >= tile_rows - half // 2 else at + half // 2
 
     def y_arrival(slot, pair):
         for at in range(2):
@@ -266,12 +306,11 @@
 
     ys_arrival(n)
 
-    @pl.loop(0, pairs)
-    def _(pair):
+    for pair in range(pairs):
         y_arrival(n, pair)
         for at, field in enumerate(widened(n, pair)):
             probe_field[2 * pair + at] = field
-            out[2 * pair + at] = jnp.zeros((tile_rows, tile_cols), F32)
+            total[2 * pair + at] = jnp.zeros((tile_rows, tile_cols), F32)
 
     blocks = wide // 128
     if slabs < SUBLANES:
@@ -287,13 +326,13 @@
 
     def load_turned(at):
         picks = [
-            turned[block, pl.ds(at % tall, SUBLANES, stride=tall), :] for block in range(blocks)
+            turned[block, pl.ds(place(at), SUBLANES, stride=tall), :] for block in range(blocks)
         ]
         return jnp.concatenate(picks, 1)
 
     def store_result(at, value):
         for block in range(tile_cols // 128):
-            result[block, pl.ds(at, SUBLANES, stride=tile_rows), :] = value[:, block * 128 : (block + 1) * 128]
+            result[block, pl.ds(result_place(at), SUBLANES, stride=tile_rows), :] = value[:, block * 128 : (block + 1) * 128]
 
     def through(buffer):
         def load(at):
@@ -322,16 +361,12 @@
             sweep(loads_now, store_now, SWEEPS - 1 - step)
             loads_now = (load_a, load_b)[step % 2]
         for pair in range(pairs):
-            head = core[slot, pair, 0].astype(F32)
-            tail = core[slot, pair, 1].astype(F32)
-            for at in range(2):
+            for at, member in enumerate(centre(slot, pair)):
                 slab = 2 * pair + at
-                cut = slice(at * half, (at + 1) * half)
-                member = jnp.concatenate([head[cut], tail[cut]], 0)
                 done = jnp.concatenate(
                     [result[block, slab * tile_rows : (slab + 1) * tile_rows] for block in range(tile_cols // 128)], 1
                 )
-                out[slab] += member * done
+                total[slab] += member * done
 
     def hand_on(slot, pair, onward):
         z_copy(slot, pair, onward).wait_recv()
@@ -386,6 +421,11 @@
         @pl.when((slot >= 0) & (slot < n) & (turn > 0))
         def _():
             add_member(slot)
+
+    for slab in range(slabs):
+        ends, middle = total[slab, :half], swap(total[slab, half:])
+        out[slab, :half] = jnp.where(low_rows, ends, middle)
+        out[slab, half:] = jnp.where(low_rows, middle, ends)
 
     @pl.loop(0, n)
     def _(slot):
@@ -437,9 +477,9 @@
             pltpu.VMEM(flat, bf16),
             pltpu.VMEM((tile_rows, tile_cols), jnp.int32),
             pltpu.SMEM(class_rate.shape, F32),
-            pltpu.VMEM((n + 1, pairs, 2, tile_rows, tile_cols), bf16),
-            pltpu.VMEM((n + 1, pairs, tile_rows, tile_cols), bf16),
-            pltpu.VMEM((n + 1, pairs, tile_rows, tile_cols), bf16),
+            pltpu.VMEM((n + 1, pairs, 4, tile_rows, tile_cols // 2), bf16),
+            pltpu.VMEM((n + 1, pairs, tile_rows, tile_cols // 2), bf16),
+            pltpu.VMEM((n + 1, pairs, tile_rows, tile_cols // 2), bf16),
             pltpu.VMEM((n + 1, tile_rows, 128), bf16),
             pltpu.VMEM((n + 1, tile_rows, 128), bf16),
             pltpu.VMEM((n + 1, tile_rows, 128), bf16),
@@ -456,6 +496,7 @@
             pltpu.VMEM((tall, SUBLANES, wide), F32),
             pltpu.VMEM((tall, SUBLANES, wide), F32),
             pltpu.VMEM((tile_cols // 128, SUBLANES * tile_rows, 128), F32),
+            pltpu.VMEM(flat, F32),
             dma((4,)), dma((n, pairs, 2)), dma((n, pairs)), dma((n, 2)), dma((n,)),
             dma((n + 1, pairs, 2)), dma((n + 1, pairs, 2)), dma((n + 1, 2)), dma((n + 1, 2)),
             dma((2,)), dma((2,)), dma((2,)), dma((2,)), dma((2,)), dma((2,)),

time: 23.8 us -> 23.3 us (0.979)
  Pallas kernels: 23 us -> 22.5 us
    pallas_call x1, Pallas kernels: 23 us -> 22.5 us  [body(): pl.pallas_call(functools.partial(kernel, n, rows, cols), out_shape=pltpu....]
where the time goes in v5:
time: 23.3 us; the launch traced here: 23.2 us
  Pallas kernels  22.5 us (97%)
  other arithmetic  0.7 us (3%)
    pallas_call x1, Pallas kernels, body(): pl.pallas_call(functools.partial(kernel, n, rows, cols), out_shape=pltpu....  22.5 us
    div x1, other arithmetic, body(): return out.reshape(pert.shape) / (n - 1)  0.7 us

profile of v5, /device:TPU:1, one launch (start us, length us, event | category | flops | bytes accessed | tf_op | source)
XLA Modules:
  0.0 23.2 jit_solution(14729798322179581450)
XLA Ops:
  0.0 22.5 %shard_map.46 = f32[6,16,512]{2,1,0:T(8,128)S(1)} custom-call(bf16[6,16,512]{2,1,0:T(8,128)(2,1)} %bitcast.3, bf16[6,16,512]{2,1,0:T(8,128)(2,1)} %bitcast.4, s32[16,512]{1,0:T(8,128)} %classes_hbm.1, f32[8]{0:T(128)} %rates_hbm.1), custom_call_target="tpu_custom_call" | custom-call | tf_op jit(solution)/shard_map/pallas_call | solution.py:470
  22.5 0.7 %broadcast_multiply_fusion = f32[6,16,512]{2,1,0:T(8,128)} fusion(f32[6,16,512]{2,1,0:T(8,128)S(1)} %shard_map.46), kind=kLoop, calls=%fused_computation | loop fusion | flops 49152 | bytes 393216 | tf_op jit(solution)/shard_map/div | solution.py:508

commit v6 on v5

--- a/solution.py
+++ b/solution.py
@@ -407,6 +407,11 @@
         at_distance(away, hand_on_side)
 
     lower = 1 - (2 * me) // n
+    ahead = has_prev + has_next
+
+    @pl.when(ahead == 2)
+    def _():
+        arrivals(1)
 
     @pl.loop(0, 2 * n)
     def _(turn):
@@ -416,7 +421,7 @@
 
         @pl.when(second == 1)
         def _():
-            arrivals(away + 1)
+            arrivals(away + ahead)
 
         @pl.when((slot >= 0) & (slot < n) & (turn > 0))
         def _():

time: 23.3 us -> 22.5 us (0.966)
  Pallas kernels: 22.5 us -> 21.7 us
    pallas_call x1, Pallas kernels: 22.5 us -> 21.7 us  [body(): pl.pallas_call(functools.partial(kernel, n, rows, cols), out_shape=pltpu....]
where the time goes in v6:
time: 22.5 us; the launch traced here: 22.4 us
  Pallas kernels  21.7 us (96%)
  other arithmetic  0.7 us (3%)
    pallas_call x1, Pallas kernels, body(): pl.pallas_call(functools.partial(kernel, n, rows, cols), out_shape=pltpu....  21.7 us
    div x1, other arithmetic, body(): return out.reshape(pert.shape) / (n - 1)  0.7 us

profile of v6, /device:TPU:1, one launch (start us, length us, event | category | flops | bytes accessed | tf_op | source)
XLA Modules:
  0.0 22.4 jit_solution(2677565589247519160)
XLA Ops:
  0.0 21.7 %shard_map.46 = f32[6,16,512]{2,1,0:T(8,128)S(1)} custom-call(bf16[6,16,512]{2,1,0:T(8,128)(2,1)} %bitcast.3, bf16[6,16,512]{2,1,0:T(8,128)(2,1)} %bitcast.4, s32[16,512]{1,0:T(8,128)} %classes_hbm.1, f32[8]{0:T(128)} %rates_hbm.1), custom_call_target="tpu_custom_call" | custom-call | tf_op jit(solution)/shard_map/pallas_call | solution.py:475
  21.7 0.7 %broadcast_multiply_fusion = f32[6,16,512]{2,1,0:T(8,128)} fusion(f32[6,16,512]{2,1,0:T(8,128)S(1)} %shard_map.46), kind=kLoop, calls=%fused_computation | loop fusion | flops 49152 | bytes 393216 | tf_op jit(solution)/shard_map/div | solution.py:513

commit v7 on v6

--- a/solution.py
+++ b/solution.py
@@ -17,10 +17,10 @@
     n, rows, cols,
     pert_hbm, probes_hbm, classes_hbm, rates_hbm, out,
     pert, probes, classes, rates,
-    core, above, below, side, side_above, side_below,
+    core, above, below,
     side_out, side_in, cls, cls_in, cls_above, cls_below,
     probe_field, keep, rate, turned, field_a, field_b, result, total,
-    in_sem, z_send, z_recv, zs_send, zs_recv, y_send, y_recv, ys_send, ys_recv,
+    in_sem, z_send, z_recv, y_send, y_recv,
     x_send, x_recv, cx_send, cx_recv, cy_send, cy_recv,
 ):
     slabs, tile_rows, tile_cols = pert.shape
@@ -76,27 +76,22 @@
             remote(classes.at[:, block : block + 128], cls_in.at[at], cx_send.at[at], cx_recv.at[at], where),
         )
 
-    def z_copy(slot, pair, at):
+    side_at = pairs * tile_rows
+    bottom_at = side_at + tile_rows
+    middle_at = bottom_at + side_at
+    parts = (pl.ds(middle_at, slabs * tile_rows), pl.ds(0, middle_at))
+    halo = side_at + tile_rows
+
+    def z_copy(slot, part, at):
         return remote(
-            core.at[slot, pair], core.at[slot, pair],
-            z_send.at[slot, pair, at], z_recv.at[slot, pair], sides[4 + at][1],
-        )
-
-    def zs_copy(slot, at):
+            core.at[slot, parts[part]], core.at[slot, parts[part]],
+            z_send.at[slot, part, at], z_recv.at[slot, part], sides[4 + at][1],
+        )
+
+    def y_copy(slot, at):
         return remote(
-            side.at[slot], side.at[slot], zs_send.at[slot, at], zs_recv.at[slot], sides[4 + at][1]
-        )
-
-    def y_copy(slot, pair, at):
-        return remote(
-            core.at[slot, pair, at], (below, above)[at].at[slot, pair],
-            y_send.at[slot, pair, at], y_recv.at[slot, pair, at], sides[at][1],
-        )
-
-    def ys_copy(slot, at):
-        return remote(
-            side.at[slot], (side_below, side_above)[at].at[slot],
-            ys_send.at[slot, at], ys_recv.at[slot, at], sides[at][1],
+            core.at[slot, pl.ds((0, side_at)[at], halo)], (below, above)[at].at[slot],
+            y_send.at[slot, at], y_recv.at[slot, at], sides[at][1],
         )
 
     def cy_copy(at):
@@ -115,38 +110,37 @@
     def swap(rows_now):
         return pltpu.roll(rows_now, half // 2, 0)
 
-    def folded(rows_now):
-        return jnp.concatenate([rows_now[:, :fold], rows_now[:, fold:]], 0).astype(jnp.bfloat16)
-
-    def unfolded(block):
-        both = block.astype(F32)
+    def keep_block(slot, first, rows_now):
+        both = jnp.concatenate([rows_now[:, :fold], rows_now[:, fold:]], 0)
+        core[slot, first : first + tile_rows] = both.astype(jnp.bfloat16)
+
+    def block_of(ref, slot, first):
+        both = ref[slot, first : first + tile_rows].astype(F32)
         return jnp.concatenate([both[:half], both[half:]], 1)
 
     def pack(which, slot):
         for pair in range(pairs):
             first = which[2 * pair].astype(F32)
             second = which[2 * pair + 1].astype(F32)
-            core[slot, pair, 0] = folded(jnp.where(low_rows, first[:half], swap(second[:half])))
-            core[slot, pair, 1] = folded(jnp.where(low_rows, swap(first[half:]), second[half:]))
+            keep_block(slot, tile_rows * pair, jnp.where(low_rows, first[:half], swap(second[:half])))
+            keep_block(slot, bottom_at + tile_rows * pair, jnp.where(low_rows, swap(first[half:]), second[half:]))
             for at, tile in enumerate((first, second)):
-                core[slot, pair, 2 + at] = folded(jnp.where(low_rows, swap(tile[:half]), swap(tile[half:])))
+                keep_block(slot, middle_at + tile_rows * (2 * pair + at), jnp.where(low_rows, swap(tile[:half]), swap(tile[half:])))
 
     def start_rows(slot):
-        for pair in range(pairs):
-            for at in range(2):
-                @if_sent(at)
-                def _(pair=pair, at=at):
-                    y_copy(slot, pair, at).start()
+        for at in range(2):
+            @if_sent(at)
+            def _(at=at):
+                y_copy(slot, at).start()
 
     loads[0].wait()
     pack(pert, me)
     pl.semaphore_wait(barrier, has_up + has_down + has_left + has_right + has_prev + has_next)
 
-    for pair in range(pairs):
-        for at in range(2):
-            @if_sent(4 + at)
-            def _(pair=pair, at=at):
-                z_copy(me, pair, at).start()
+    for at in range(2):
+        @if_sent(4 + at)
+        def _(at=at):
+            z_copy(me, 0, at).start()
 
     for load in loads[1:]:
         load.wait()
@@ -174,20 +168,16 @@
                 copy.start()
 
     pack(probes, n)
-    start_rows(n)
-    start_rows(me)
     cls[:, 0:tile_cols] = classes[...]
 
     @pl.when(has_up == 0)
     def _():
         above[...] = jnp.zeros_like(above)
-        side_above[...] = jnp.zeros_like(side_above)
         cls_above[...] = jnp.full_like(cls_above, -1)
 
     @pl.when(has_down == 0)
     def _():
         below[...] = jnp.zeros_like(below)
-        side_below[...] = jnp.zeros_like(side_below)
         cls_below[...] = jnp.full_like(cls_below, -1)
 
     @pl.when(has_right == 0)
@@ -208,40 +198,46 @@
 
     for at, slot in enumerate((me, n)):
         merged = jnp.where(lane < 64, side_in[0, at].astype(F32), side_in[1, at].astype(F32))
-        side[slot] = merged.astype(jnp.bfloat16)
+        core[slot, side_at:bottom_at] = jnp.concatenate([merged] * (fold // 128), 1).astype(jnp.bfloat16)
+
+    for at in range(2):
+        @if_sent(4 + at)
+        def _(at=at):
+            z_copy(me, 1, at).start()
+    start_rows(n)
+    start_rows(me)
+
     cls[:, tile_cols:wide] = jnp.where(lane < 64, cls_in[0], cls_in[1])
-
-    for slot in (n, me):
-        for at in range(2):
-            @if_sent(at)
-            def _(slot=slot, at=at):
-                ys_copy(slot, at).start()
-
     for at in range(2):
         @if_sent(at)
         def _(at=at):
             cy_copy(at).start()
-
-    for at in range(2):
-        @if_sent(4 + at)
-        def _(at=at):
-            zs_copy(me, at).start()
 
     lane_tall = lax.broadcasted_iota(jnp.int32, (tall, 128), 1) < 64
 
     def place(at):
         return at + half if at < 0 else at if at < half // 2 else at + half // 2
 
+    def top_of(slot, pair):
+        return block_of(core, slot, tile_rows * pair)
+
+    def bottom_of(slot, pair):
+        return block_of(core, slot, bottom_at + tile_rows * pair)
+
+    def middle_of(slot, pair, at):
+        return block_of(core, slot, middle_at + tile_rows * (2 * pair + at))
+
     def widened(slot, pair):
-        top, bottom = unfolded(core[slot, pair, 0]), unfolded(core[slot, pair, 1])
-        over, under = unfolded(above[slot, pair]), unfolded(below[slot, pair])
-        beside_own = side[slot].astype(F32)
+        top, bottom = top_of(slot, pair), bottom_of(slot, pair)
+        over = block_of(above, slot, tile_rows * (1 + pair))
+        under = block_of(below, slot, tile_rows * pair)
+        beside_own = core[slot, side_at:bottom_at, 0:128].astype(F32)
         ends, middle = beside_own[:half], beside_own[half:]
         beside = jnp.concatenate(
             [
-                jnp.where(low_side, ends, side_above[slot].astype(F32)[:half]),
+                jnp.where(low_side, ends, above[slot, 0:tile_rows, 0:128].astype(F32)[:half]),
                 middle,
-                swap(jnp.where(low_side, side_below[slot].astype(F32)[:half], ends)),
+                swap(jnp.where(low_side, below[slot, side_at:halo, 0:128].astype(F32)[:half], ends)),
             ],
             0,
         )
@@ -254,7 +250,7 @@
             else:
                 head = jnp.where(low_rows, swap(top), over)
                 tail = jnp.where(low_rows, swap(bottom), under)
-            mine = jnp.concatenate([head, unfolded(core[slot, pair, 2 + at]), tail], 0)
+            mine = jnp.concatenate([head, middle_of(slot, pair, at), tail], 0)
             end = jnp.where(
                 lane_tall,
                 pltpu.roll(beside, (128 - low) % 128, 1) if low else beside,
@@ -264,9 +260,9 @@
         return both
 
     def centre(slot, pair):
-        top, bottom = unfolded(core[slot, pair, 0]), unfolded(core[slot, pair, 1])
+        top, bottom = top_of(slot, pair), bottom_of(slot, pair)
         return [
-            jnp.concatenate([ends, unfolded(core[slot, pair, 2 + at])], 0)
+            jnp.concatenate([ends, middle_of(slot, pair, at)], 0)
             for at, ends in enumerate(
                 (jnp.where(low_rows, top, swap(bottom)), jnp.where(low_rows, swap(top), bottom))
             )
@@ -277,17 +273,11 @@
             return at
         return at - half if at >= tile_rows - half // 2 else at + half // 2
 
-    def y_arrival(slot, pair):
+    def y_arrival(slot):
         for at in range(2):
             @if_sent(1 - at)
             def _(at=at):
-                y_copy(slot, pair, at).wait_recv()
-
-    def ys_arrival(slot):
-        for at in range(2):
-            @if_sent(1 - at)
-            def _(at=at):
-                ys_copy(slot, at).wait_recv()
+                y_copy(slot, at).wait_recv()
 
     for at in range(2):
         @if_sent(1 - at)
@@ -304,10 +294,8 @@
         rate[at] = line
         keep[at] = 1.0 - 4.0 * line
 
-    ys_arrival(n)
-
+    y_arrival(n)
     for pair in range(pairs):
-        y_arrival(n, pair)
         for at, field in enumerate(widened(n, pair)):
             probe_field[2 * pair + at] = field
             total[2 * pair + at] = jnp.zeros((tile_rows, tile_cols), F32)
@@ -344,9 +332,7 @@
         return load, store
 
     def add_member(slot):
-        for pair in range(pairs):
-            y_arrival(slot, pair)
-        ys_arrival(slot)
+        y_arrival(slot)
         for pair in range(pairs):
             for at, member in enumerate(widened(slot, pair)):
                 slab = 2 * pair + at
@@ -368,29 +354,15 @@
                 )
                 total[slab] += member * done
 
-    def hand_on(slot, pair, onward):
-        z_copy(slot, pair, onward).wait_recv()
+    def hand_on(slot, part, onward):
+        z_copy(slot, part, onward).wait_recv()
 
         @if_sent(4 + onward)
         def _():
-            z_copy(slot, pair, onward).start()
-
-        for at in range(2):
-            @if_sent(at)
-            def _(at=at):
-                y_copy(slot, pair, at).start()
-
-    def hand_on_side(slot, onward):
-        zs_copy(slot, onward).wait_recv()
-
-        @if_sent(4 + onward)
-        def _():
-            zs_copy(slot, onward).start()
-
-        for at in range(2):
-            @if_sent(at)
-            def _(at=at):
-                ys_copy(slot, at).start()
+            z_copy(slot, part, onward).start()
+
+        if part:
+            start_rows(slot)
 
     def at_distance(away, act):
         @pl.when(me - away >= 0)
@@ -402,9 +374,8 @@
             act(me + away, 0)
 
     def arrivals(away):
-        for pair in range(pairs):
-            at_distance(away, lambda slot, onward: hand_on(slot, pair, onward))
-        at_distance(away, hand_on_side)
+        for part in range(len(parts)):
+            at_distance(away, lambda slot, onward: hand_on(slot, part, onward))
 
     lower = 1 - (2 * me) // n
     ahead = has_prev + has_next
@@ -437,18 +408,15 @@
         for at in range(2):
             @pl.when((sides[4 + at][0] == 1) & ((slot >= me) if at == 0 else (slot <= me)))
             def _(at=at):
-                for pair in range(pairs):
-                    z_copy(slot, pair, at).wait_send()
-                zs_copy(slot, at).wait_send()
+                for part in range(len(parts)):
+                    z_copy(slot, part, at).wait_send()
 
     @pl.loop(0, n + 1)
     def _(slot):
         for at in range(2):
             @if_sent(at)
             def _(at=at):
-                for pair in range(pairs):
-                    y_copy(slot, pair, at).wait_send()
-                ys_copy(slot, at).wait_send()
+                y_copy(slot, at).wait_send()
 
     for at in range(2):
         @if_sent(at)
@@ -482,12 +450,9 @@
             pltpu.VMEM(flat, bf16),
             pltpu.VMEM((tile_rows, tile_cols), jnp.int32),
             pltpu.SMEM(class_rate.shape, F32),
-            pltpu.VMEM((n + 1, pairs, 4, tile_rows, tile_cols // 2), bf16),
-            pltpu.VMEM((n + 1, pairs, tile_rows, tile_cols // 2), bf16),
-            pltpu.VMEM((n + 1, pairs, tile_rows, tile_cols // 2), bf16),
-            pltpu.VMEM((n + 1, tile_rows, 128), bf16),
-            pltpu.VMEM((n + 1, tile_rows, 128), bf16),
-            pltpu.VMEM((n + 1, tile_rows, 128), bf16),
+            pltpu.VMEM((n + 1, (4 * pairs + 1) * tile_rows, tile_cols // 2), bf16),
+            pltpu.VMEM((n + 1, (pairs + 1) * tile_rows, tile_cols // 2), bf16),
+            pltpu.VMEM((n + 1, (pairs + 1) * tile_rows, tile_cols // 2), bf16),
             pltpu.VMEM((2, 2, tile_rows, 128), bf16),
             pltpu.VMEM((2, 2, tile_rows, 128), bf16),
             pltpu.VMEM((tile_rows, wide), jnp.int32),
@@ -502,8 +467,7 @@
             pltpu.VMEM((tall, SUBLANES, wide), F32),
             pltpu.VMEM((tile_cols // 128, SUBLANES * tile_rows, 128), F32),
             pltpu.VMEM(flat, F32),
-            dma((4,)), dma((n, pairs, 2)), dma((n, pairs)), dma((n, 2)), dma((n,)),
-            dma((n + 1, pairs, 2)), dma((n + 1, pairs, 2)), dma((n + 1, 2)), dma((n + 1, 2)),
+            dma((4,)), dma((n, 2, 2)), dma((n, 2)), dma((n + 1, 2)), dma((n + 1, 2)),
             dma((2,)), dma((2,)), dma((2,)), dma((2,)), dma((2,)), dma((2,)),
         ],
         compiler_params=pltpu.CompilerParams(

time: 22.5 us -> 23.6 us (1.049)
  Pallas kernels: 21.7 us -> 22.8 us
    pallas_call x1, Pallas kernels: 21.7 us -> 22.8 us  [body(): pl.pallas_call(functools.partial(kernel, n, rows, cols), out_shape=pltpu....]
where the time goes in v7:
time: 23.6 us; the launch traced here: 23.5 us
  Pallas kernels  22.8 us (97%)
  other arithmetic  0.7 us (3%)
    pallas_call x1, Pallas kernels, body(): pl.pallas_call(functools.partial(kernel, n, rows, cols), out_shape=pltpu....  22.8 us
    div x1, other arithmetic, body(): return out.reshape(pert.shape) / (n - 1)  0.7 us

profile of v7, /device:TPU:1, one launch (start us, length us, event | category | flops | bytes accessed | tf_op | source)
XLA Modules:
  0.0 23.5 jit_solution(10829001258806435099)
XLA Ops:
  0.0 22.8 %shard_map.46 = f32[6,16,512]{2,1,0:T(8,128)S(1)} custom-call(bf16[6,16,512]{2,1,0:T(8,128)(2,1)} %bitcast.3, bf16[6,16,512]{2,1,0:T(8,128)(2,1)} %bitcast.4, s32[16,512]{1,0:T(8,128)} %classes_hbm.1, f32[8]{0:T(128)} %rates_hbm.1), custom_call_target="tpu_custom_call" | custom-call | tf_op jit(solution)/shard_map/pallas_call | solution.py:443
  22.8 0.7 %broadcast_multiply_fusion = f32[6,16,512]{2,1,0:T(8,128)} fusion(f32[6,16,512]{2,1,0:T(8,128)S(1)} %shard_map.46), kind=kLoop, calls=%fused_computation | loop fusion | flops 49152 | bytes 393216 | tf_op jit(solution)/shard_map/div | solution.py:477

commit v8 on v7

--- a/solution.py
+++ b/solution.py
@@ -133,16 +133,7 @@
             def _(at=at):
                 y_copy(slot, at).start()
 
-    loads[0].wait()
-    pack(pert, me)
-    pl.semaphore_wait(barrier, has_up + has_down + has_left + has_right + has_prev + has_next)
-
-    for at in range(2):
-        @if_sent(4 + at)
-        def _(at=at):
-            z_copy(me, 0, at).start()
-
-    for load in loads[1:]:
+    for load in loads:
         load.wait()
     lane = lax.broadcasted_iota(jnp.int32, (tile_rows, 128), 1)
     for at, which in enumerate((pert, probes)):
@@ -161,11 +152,19 @@
             ends = jnp.where(low_side, rim[:half], rim[half:])
             middle = jnp.where(low_side, swap(rim[:half]), swap(rim[half:]))
             side_out[way, at] = jnp.concatenate([ends, middle], 0).astype(jnp.bfloat16)
+    pack(pert, me)
+    pl.semaphore_wait(barrier, has_up + has_down + has_left + has_right + has_prev + has_next)
+
     for at in range(2):
         @if_sent(2 + at)
         def _(at=at):
             for copy in x_copies(at):
                 copy.start()
+
+    for at in range(2):
+        @if_sent(4 + at)
+        def _(at=at):
+            z_copy(me, 0, at).start()
 
     pack(probes, n)
     cls[:, 0:tile_cols] = classes[...]
@@ -388,7 +387,7 @@
     def _(turn):
         away = turn // 2
         second = turn % 2
-        slot = me + away * (2 * ((second + lower) % 2) - 1)
+        slot = me + away * (1 - 2 * ((second + lower) % 2))
 
         @pl.when(second == 1)
         def _():

time: 23.6 us -> 22.2 us (0.941)
  Pallas kernels: 22.8 us -> 21.3 us
    pallas_call x1, Pallas kernels: 22.8 us -> 21.3 us  [body(): pl.pallas_call(functools.partial(kernel, n, rows, cols), out_shape=pltpu....]
where the time goes in v8:
time: 22.2 us; the launch traced here: 22 us
  Pallas kernels  21.3 us (96%)
  other arithmetic  0.7 us (3%)
    pallas_call x1, Pallas kernels, body(): pl.pallas_call(functools.partial(kernel, n, rows, cols), out_shape=pltpu....  21.3 us
    div x1, other arithmetic, body(): return out.reshape(pert.shape) / (n - 1)  0.7 us

profile of v8, /device:TPU:1, one launch (start us, length us, event | category | flops | bytes accessed | tf_op | source)
XLA Modules:
  0.0 22.0 jit_solution(15979022793580131542)
XLA Ops:
  0.0 21.3 %shard_map.46 = f32[6,16,512]{2,1,0:T(8,128)S(1)} custom-call(bf16[6,16,512]{2,1,0:T(8,128)(2,1)} %bitcast.3, bf16[6,16,512]{2,1,0:T(8,128)(2,1)} %bitcast.4, s32[16,512]{1,0:T(8,128)} %classes_hbm.1, f32[8]{0:T(128)} %rates_hbm.1), custom_call_target="tpu_custom_call" | custom-call | tf_op jit(solution)/shard_map/pallas_call | solution.py:442
  21.3 0.7 %broadcast_multiply_fusion = f32[6,16,512]{2,1,0:T(8,128)} fusion(f32[6,16,512]{2,1,0:T(8,128)S(1)} %shard_map.46), kind=kLoop, calls=%fused_computation | loop fusion | flops 49152 | bytes 393216 | tf_op jit(solution)/shard_map/div | solution.py:476

commit v9 on v8

--- a/solution.py
+++ b/solution.py
@@ -20,7 +20,7 @@
     core, above, below,
     side_out, side_in, cls, cls_in, cls_above, cls_below,
     probe_field, keep, rate, turned, field_a, field_b, result, total,
-    in_sem, z_send, z_recv, y_send, y_recv,
+    in_sem, z_send, z_far, z_recv, y_send, y_recv,
     x_send, x_recv, cx_send, cx_recv, cy_send, cy_recv,
 ):
     slabs, tile_rows, tile_cols = pert.shape
@@ -47,6 +47,8 @@
     has_right = 1 - (col + 1) // cols
     has_prev = (me + n - 1) // n
     has_next = 1 - (me + 1) // n
+    has_prev2 = (me + n - 2) // n
+    has_next2 = 1 - (me + 2) // n
     sides = (
         (has_up, {"row": row - 1}),
         (has_down, {"row": row + 1}),
@@ -54,6 +56,8 @@
         (has_right, {"col": col + 1}),
         (has_prev, {"member": me - 1}),
         (has_next, {"member": me + 1}),
+        (has_prev2, {"member": me - 2}),
+        (has_next2, {"member": me + 2}),
     )
 
     barrier = pltpu.get_barrier_semaphore()
@@ -87,6 +91,22 @@
             core.at[slot, parts[part]], core.at[slot, parts[part]],
             z_send.at[slot, part, at], z_recv.at[slot, part], sides[4 + at][1],
         )
+
+    def z_far_copy(part, at):
+        return remote(
+            core.at[me, parts[part]], core.at[me, parts[part]],
+            z_far.at[part, at], z_recv.at[me, part], sides[6 + at][1],
+        )
+
+    def z_start(part):
+        for at in range(2):
+            @if_sent(6 + at)
+            def _(at=at):
+                z_far_copy(part, at).start()
+        for at in range(2):
+            @if_sent(4 + at)
+            def _(at=at):
+                z_copy(me, part, at).start()
 
     def y_copy(slot, at):
         return remote(
@@ -153,7 +173,7 @@
             middle = jnp.where(low_side, swap(rim[:half]), swap(rim[half:]))
             side_out[way, at] = jnp.concatenate([ends, middle], 0).astype(jnp.bfloat16)
     pack(pert, me)
-    pl.semaphore_wait(barrier, has_up + has_down + has_left + has_right + has_prev + has_next)
+    pl.semaphore_wait(barrier, has_up + has_down + has_left + has_right + has_prev + has_next + has_prev2 + has_next2)
 
     for at in range(2):
         @if_sent(2 + at)
@@ -161,10 +181,7 @@
             for copy in x_copies(at):
                 copy.start()
 
-    for at in range(2):
-        @if_sent(4 + at)
-        def _(at=at):
-            z_copy(me, 0, at).start()
+    z_start(0)
 
     pack(probes, n)
     cls[:, 0:tile_cols] = classes[...]
@@ -199,10 +216,7 @@
         merged = jnp.where(lane < 64, side_in[0, at].astype(F32), side_in[1, at].astype(F32))
         core[slot, side_at:bottom_at] = jnp.concatenate([merged] * (fold // 128), 1).astype(jnp.bfloat16)
 
-    for at in range(2):
-        @if_sent(4 + at)
-        def _(at=at):
-            z_copy(me, 1, at).start()
+    z_start(1)
     start_rows(n)
     start_rows(me)
 
@@ -353,10 +367,10 @@
                 )
                 total[slab] += member * done
 
-    def hand_on(slot, part, onward):
+    def hand_on(slot, part, onward, away):
         z_copy(slot, part, onward).wait_recv()
 
-        @if_sent(4 + onward)
+        @pl.when((sides[4 + onward][0] == 1) & (away >= 2))
         def _():
             z_copy(slot, part, onward).start()
 
@@ -374,7 +388,7 @@
 
     def arrivals(away):
         for part in range(len(parts)):
-            at_distance(away, lambda slot, onward: hand_on(slot, part, onward))
+            at_distance(away, lambda slot, onward: hand_on(slot, part, onward, away))
 
     lower = 1 - (2 * me) // n
     ahead = has_prev + has_next
@@ -405,10 +419,19 @@
     @pl.loop(0, n)
     def _(slot):
         for at in range(2):
-            @pl.when((sides[4 + at][0] == 1) & ((slot >= me) if at == 0 else (slot <= me)))
+            @pl.when(
+                (sides[4 + at][0] == 1)
+                & ((slot == me) | ((slot >= me + 2) if at == 0 else (slot <= me - 2)))
+            )
             def _(at=at):
                 for part in range(len(parts)):
                     z_copy(slot, part, at).wait_send()
+
+    for at in range(2):
+        @if_sent(6 + at)
+        def _(at=at):
+            for part in range(len(parts)):
+                z_far_copy(part, at).wait_send()
 
     @pl.loop(0, n + 1)
     def _(slot):
@@ -466,7 +489,7 @@
             pltpu.VMEM((tall, SUBLANES, wide), F32),
             pltpu.VMEM((tile_cols // 128, SUBLANES * tile_rows, 128), F32),
             pltpu.VMEM(flat, F32),
-            dma((4,)), dma((n, 2, 2)), dma((n, 2)), dma((n + 1, 2)), dma((n + 1, 2)),
+            dma((4,)), dma((n, 2, 2)), dma((2, 2)), dma((n, 2)), dma((n + 1, 2)), dma((n + 1, 2)),
             dma((2,)), dma((2,)), dma((2,)), dma((2,)), dma((2,)), dma((2,)),
         ],
         compiler_params=pltpu.CompilerParams(

time: 22.2 us -> 21.5 us (0.968)
  Pallas kernels: 21.3 us -> 20.6 us
    pallas_call x1, Pallas kernels: 21.3 us -> 20.6 us  [body(): pl.pallas_call(functools.partial(kernel, n, rows, cols), out_shape=pltpu....]
where the time goes in v9:
time: 21.5 us; the launch traced here: 21.3 us
  Pallas kernels  20.6 us (96%)
  other arithmetic  0.7 us (3%)
    pallas_call x1, Pallas kernels, body(): pl.pallas_call(functools.partial(kernel, n, rows, cols), out_shape=pltpu....  20.6 us
    div x1, other arithmetic, body(): return out.reshape(pert.shape) / (n - 1)  0.7 us

profile of v9, /device:TPU:1, one launch (start us, length us, event | category | flops | bytes accessed | tf_op | source)
XLA Modules:
  0.0 21.3 jit_solution(4165601021871823584)
XLA Ops:
  0.0 20.6 %shard_map.46 = f32[6,16,512]{2,1,0:T(8,128)S(1)} custom-call(bf16[6,16,512]{2,1,0:T(8,128)(2,1)} %bitcast.3, bf16[6,16,512]{2,1,0:T(8,128)(2,1)} %bitcast.4, s32[16,512]{1,0:T(8,128)} %classes_hbm.1, f32[8]{0:T(128)} %rates_hbm.1), custom_call_target="tpu_custom_call" | custom-call | tf_op jit(solution)/shard_map/pallas_call | solution.py:465
  20.6 0.7 %broadcast_multiply_fusion = f32[6,16,512]{2,1,0:T(8,128)} fusion(f32[6,16,512]{2,1,0:T(8,128)S(1)} %shard_map.46), kind=kLoop, calls=%fused_computation | loop fusion | flops 49152 | bytes 393216 | tf_op jit(solution)/shard_map/div | solution.py:499

commit v10 on v9

--- a/solution.py
+++ b/solution.py
@@ -391,11 +391,6 @@
             at_distance(away, lambda slot, onward: hand_on(slot, part, onward, away))
 
     lower = 1 - (2 * me) // n
-    ahead = has_prev + has_next
-
-    @pl.when(ahead == 2)
-    def _():
-        arrivals(1)
 
     @pl.loop(0, 2 * n)
     def _(turn):
@@ -403,9 +398,9 @@
         second = turn % 2
         slot = me + away * (1 - 2 * ((second + lower) % 2))
 
-        @pl.when(second == 1)
+        @pl.when(second == 0)
         def _():
-            arrivals(away + ahead)
+            arrivals(away + 1)
 
         @pl.when((slot >= 0) & (slot < n) & (turn > 0))
         def _():

time: 21.5 us -> 22.5 us (1.047)
  Pallas kernels: 20.6 us -> 21.7 us
    pallas_call x1, Pallas kernels: 20.6 us -> 21.7 us  [body(): pl.pallas_call(functools.partial(kernel, n, rows, cols), out_shape=pltpu....]
where the time goes in v10:
time: 22.5 us; the launch traced here: 22.4 us
  Pallas kernels  21.7 us (96%)
  other arithmetic  0.7 us (3%)
    pallas_call x1, Pallas kernels, body(): pl.pallas_call(functools.partial(kernel, n, rows, cols), out_shape=pltpu....  21.7 us
    div x1, other arithmetic, body(): return out.reshape(pert.shape) / (n - 1)  0.7 us

profile of v10, /device:TPU:1, one launch (start us, length us, event | category | flops | bytes accessed | tf_op | source)
XLA Modules:
  0.0 22.4 jit_solution(14298046392847255213)
XLA Ops:
  0.0 21.7 %shard_map.46 = f32[6,16,512]{2,1,0:T(8,128)S(1)} custom-call(bf16[6,16,512]{2,1,0:T(8,128)(2,1)} %bitcast.3, bf16[6,16,512]{2,1,0:T(8,128)(2,1)} %bitcast.4, s32[16,512]{1,0:T(8,128)} %classes_hbm.1, f32[8]{0:T(128)} %rates_hbm.1), custom_call_target="tpu_custom_call" | custom-call | tf_op jit(solution)/shard_map/pallas_call | solution.py:460
  21.7 0.7 %broadcast_multiply_fusion = f32[6,16,512]{2,1,0:T(8,128)} fusion(f32[6,16,512]{2,1,0:T(8,128)S(1)} %shard_map.46), kind=kLoop, calls=%fused_computation | loop fusion | flops 49152 | bytes 393216 | tf_op jit(solution)/shard_map/div | solution.py:494

commit v11 on v9

--- a/solution.py
+++ b/solution.py
@@ -403,9 +403,12 @@
         second = turn % 2
         slot = me + away * (1 - 2 * ((second + lower) % 2))
 
-        @pl.when(second == 1)
+        early = (second == 1) & ((ahead == 2) | (away != n - 2))
+        last = (second == 0) & (ahead == 1) & (away == n - 1)
+
+        @pl.when(early | last)
         def _():
-            arrivals(away + ahead)
+            arrivals(away + ahead + second - 1)
 
         @pl.when((slot >= 0) & (slot < n) & (turn > 0))
         def _():

time: 21.5 us -> 21.5 us (level)
  no operation moved by 1% of the time
where the time goes in v11:
time: 21.5 us; the launch traced here: 21.4 us
  Pallas kernels  20.7 us (96%)
  other arithmetic  0.7 us (3%)
    pallas_call x1, Pallas kernels, body(): pl.pallas_call(functools.partial(kernel, n, rows, cols), out_shape=pltpu....  20.7 us
    div x1, other arithmetic, body(): return out.reshape(pert.shape) / (n - 1)  0.7 us

profile of v11, /device:TPU:1, one launch (start us, length us, event | category | flops | bytes accessed | tf_op | source)
XLA Modules:
  0.0 21.4 jit_solution(15380515961213261301)
XLA Ops:
  0.0 20.7 %shard_map.46 = f32[6,16,512]{2,1,0:T(8,128)S(1)} custom-call(bf16[6,16,512]{2,1,0:T(8,128)(2,1)} %bitcast.3, bf16[6,16,512]{2,1,0:T(8,128)(2,1)} %bitcast.4, s32[16,512]{1,0:T(8,128)} %classes_hbm.1, f32[8]{0:T(128)} %rates_hbm.1), custom_call_target="tpu_custom_call" | custom-call | tf_op jit(solution)/shard_map/pallas_call | solution.py:468
  20.7 0.7 %broadcast_multiply_fusion = f32[6,16,512]{2,1,0:T(8,128)} fusion(f32[6,16,512]{2,1,0:T(8,128)S(1)} %shard_map.46), kind=kLoop, calls=%fused_computation | loop fusion | flops 49152 | bytes 393216 | tf_op jit(solution)/shard_map/div | solution.py:502
